TPU v7x, 512 devices: a whole 4x8x8 slice. The times are simulated.
512 devices in a mesh: row: 32 (over x, z), col: 16 (over y, core).
Axes of the slice: x: 4, y: 8, z: 8, core: 2. Of those that a mesh axis runs over, the one named last changes fastest.
Arguments:
- object_field: float32 [2, 4096, 2048], P(None, 'row', 'col'), may hold values from -6 to 6
- amplitudes: bfloat16 [32, 16, 12, 128, 128], P('row', 'col'), may hold values from 0 to 2
- counts: int32 [32, 16], P('row', 'col'), may hold values from 1 to 12, as said below
- offsets: int32 [32, 16, 12, 2], P('row', 'col'), may hold values from 0 to 127
- mode_index: int32 [32, 16, 12], P('row', 'col'), may hold values from 0 to 15
- mix_table: float32 [16, 4], replicated, may hold values from -1 to 1
- probe_modes: float32 [4, 2, 128, 128], replicated, may hold values from -6 to 6
Outputs:
- new_object: float32 [2, 4096, 2048], P(None, 'row', 'col')
- new_modes: float32 [4, 2, 128, 128], replicated
Inputs may be any that keep to these rules, and one draw needn't show every extreme that they name: `counts`: some tile lists exactly 12 positions and some tile exactly one; the others list between 6 and 12.
All inputs are finite; a program needn't handle non-finite values.
Results may differ from a plain program's by a relative error of at most 0.0009.
The roundings to bfloat16 on the way count: a program that leaves them out, or rounds other values in their place, can miss the bound.
Values sent between devices are 32-bit elements; how exact they have to be, the bound alone decides.
A program may use at most 64 MiB of HBM per device.

v0:
```python
import math

import jax
import jax.numpy as jnp
from jax import lax
from jax.sharding import PartitionSpec as P

FLOOR = 0.25
RELAX = 0.5
EPSILON = 1e-06


def padded(block, sides, width):
    for axis, dim in sides:
        count = lax.axis_size(axis)
        forward = [(i, i + 1) for i in range(count - 1)]
        backward = [(target, source) for source, target in forward]
        low = lax.ppermute(
            lax.slice_in_dim(block, block.shape[dim] - width, None, axis=dim), axis, forward
        )
        high = lax.ppermute(lax.slice_in_dim(block, 0, width, axis=dim), axis, backward)
        block = jnp.concatenate([low, block, high], axis=dim)
    return block


def tables(size):
    index = jnp.arange(size, dtype=jnp.int32)
    product = index[:, None] * index[None, :] % size
    angle = product.astype(jnp.float32) * (2.0 * math.pi / size)
    factor = 1.0 / math.sqrt(size)
    return (
        (jnp.cos(angle) * factor).astype(jnp.bfloat16),
        (jnp.sin(angle) * factor).astype(jnp.bfloat16),
    )


def left_apply(cosine, sine, real, imag, sign):
    size = real.shape[0]
    stacked = jnp.dot(
        jnp.concatenate([cosine, sine], 0),
        jnp.concatenate([real, imag], 1),
        preferred_element_type=jnp.float32,
    )
    out_real = stacked[:size, :size] - sign * stacked[size:, size:]
    out_imag = stacked[:size, size:] + sign * stacked[size:, :size]
    return (out_real, out_imag)


def right_apply(cosine, sine, real, imag, sign):
    size = real.shape[0]
    stacked = jnp.dot(
        jnp.concatenate([real, imag], 0),
        jnp.concatenate([cosine, sine], 1),
        preferred_element_type=jnp.float32,
    )
    out_real = stacked[:size, :size] - sign * stacked[size:, size:]
    out_imag = stacked[size:, :size] + sign * stacked[:size, size:]
    return (out_real, out_imag)


def mix_probe(weights, modes):
    real = weights[0] * modes[0, 0]
    imag = weights[0] * modes[0, 1]
    for k in range(1, modes.shape[0]):
        real = real + weights[k] * modes[k, 0]
        imag = imag + weights[k] * modes[k, 1]
    return (real, imag)


def exit_change(patch, probe_real, probe_imag, amp, cosine, sine):
    psi_real = probe_real * patch[0] - probe_imag * patch[1]
    psi_imag = probe_real * patch[1] + probe_imag * patch[0]
    front_real, front_imag = left_apply(
        cosine, sine, psi_real.astype(jnp.bfloat16), psi_imag.astype(jnp.bfloat16), -1.0
    )
    spec_real, spec_imag = right_apply(
        cosine, sine, front_real.astype(jnp.bfloat16), front_imag.astype(jnp.bfloat16), -1.0
    )
    magnitude = jnp.sqrt(spec_real * spec_real + spec_imag * spec_imag)
    ratio = amp.astype(jnp.float32) / jnp.maximum(magnitude, FLOOR)
    fixed_real = (spec_real * ratio).astype(jnp.bfloat16)
    fixed_imag = (spec_imag * ratio).astype(jnp.bfloat16)
    back_real, back_imag = left_apply(cosine, sine, fixed_real, fixed_imag, 1.0)
    out_real, out_imag = right_apply(
        cosine, sine, back_real.astype(jnp.bfloat16), back_imag.astype(jnp.bfloat16), 1.0
    )
    return (out_real - psi_real, out_imag - psi_imag)


def position_terms(patch, weights, modes, amp, cosine, sine):
    probe_real, probe_imag = mix_probe(weights, modes)
    delta_real, delta_imag = exit_change(patch, probe_real, probe_imag, amp, cosine, sine)
    object_piece = jnp.stack(
        [
            probe_real * delta_real + probe_imag * delta_imag,
            probe_real * delta_imag - probe_imag * delta_real,
            probe_real * probe_real + probe_imag * probe_imag,
        ]
    )
    mode_piece = jnp.stack(
        [
            patch[0] * delta_real + patch[1] * delta_imag,
            patch[0] * delta_imag - patch[1] * delta_real,
            patch[0] * patch[0] + patch[1] * patch[1],
        ]
    )
    factor = jnp.stack([weights, weights, weights * weights], 1)
    return (object_piece, factor[:, :, None, None] * mode_piece[None])


def orthonormal_sequential(flat, reduce_value, count):
    basis = []
    for k in range(flat.shape[0]):
        vec_real, vec_imag = (flat[k, 0], flat[k, 1])
        if basis:
            parts = []
            for base_real, base_imag in basis:
                parts.append(jnp.sum(base_real * vec_real + base_imag * vec_imag))
                parts.append(jnp.sum(base_real * vec_imag - base_imag * vec_real))
            coeffs = reduce_value(jnp.stack(parts)) / count
            for j in range(len(basis)):
                base_real, base_imag = basis[j]
                coef_real, coef_imag = (coeffs[2 * j], coeffs[2 * j + 1])
                vec_real = vec_real - (coef_real * base_real - coef_imag * base_imag)
                vec_imag = vec_imag - (coef_real * base_imag + coef_imag * base_real)
        length = reduce_value(jnp.sum(vec_real * vec_real + vec_imag * vec_imag)) / count
        scale = 1.0 / jnp.sqrt(length + EPSILON)
        basis.append((vec_real * scale, vec_imag * scale))
    return jnp.stack([jnp.stack([pair[0], pair[1]]) for pair in basis])


def orthonormal(flat, reduce_value, count):
    return orthonormal_sequential(flat, reduce_value, count)


def local_total(values):
    return values


def body(object_field, amplitudes, counts, offsets, mode_index, mix_table, probe_modes):
    modes = probe_modes.shape[0]
    frame = probe_modes.shape[-1]
    half = frame // 2
    tile = object_field.shape[-1]
    mixes = mix_table.shape[0]
    cosine, sine = tables(frame)
    zero = jnp.zeros((), jnp.int32)
    extended = padded(object_field, (("row", 1), ("col", 2)), half)
    margins = jnp.zeros((3, tile + 2 * half, tile + 2 * half), jnp.float32)
    sums = jnp.zeros((modes, 3, frame, frame), jnp.float32)
    local_amps = amplitudes[0, 0]

    def visit(slot, carry):
        margin_acc, sum_acc = carry
        top = offsets[0, 0, slot, 0]
        left = offsets[0, 0, slot, 1]
        patch = lax.dynamic_slice(extended, (zero, top, left), (2, frame, frame))
        choose = (jnp.arange(mixes, dtype=jnp.int32) == mode_index[0, 0, slot]).astype(jnp.float32)
        weights = jnp.dot(choose, mix_table, precision=lax.Precision.HIGHEST)
        amp = lax.dynamic_index_in_dim(local_amps, slot, 0, keepdims=False)
        object_piece, mode_piece = position_terms(patch, weights, probe_modes, amp, cosine, sine)
        current = lax.dynamic_slice(margin_acc, (zero, top, left), (3, frame, frame))
        margin_acc = lax.dynamic_update_slice(margin_acc, current + object_piece, (zero, top, left))
        return (margin_acc, sum_acc + mode_piece)

    margins, sums = lax.fori_loop(zero, counts[0, 0], visit, (margins, sums))
    band = margins[:, half : half + tile, :]
    rims = jnp.concatenate([margins[:, :half, :], margins[:, half + tile :, :]], 1)
    widened = padded(rims, (("row", 1),), half)
    band = band.at[:, :half, :].add(widened[:, :half, :])
    band = band.at[:, tile - half :, :].add(widened[:, 3 * half :, :])
    sides = jnp.concatenate([band[:, :, :half], band[:, :, half + tile :]], 2)
    heightened = padded(sides, (("col", 2),), half)
    inner = band[:, :, half : half + tile]
    inner = inner.at[:, :, :half].add(heightened[:, :, :half])
    inner = inner.at[:, :, tile - half :].add(heightened[:, :, 3 * half :])
    new_object = object_field + inner[:2] / (inner[2] + RELAX)
    count = float(frame * frame)
    totals = lax.psum(sums, ("row", "col"))
    fresh = probe_modes + totals[:, :2] / (totals[:, 2:3] + RELAX)
    ortho = orthonormal(fresh.reshape(modes, 2, frame * frame), local_total, count)
    new_modes = ortho.reshape(probe_modes.shape)
    return (new_object, new_modes)


def solution(mesh):
    return jax.shard_map(
        body,
        mesh=mesh,
        in_specs=(
            P(None, "row", "col"),
            P("row", "col", None, None, None),
            P("row", "col"),
            P("row", "col", None, None),
            P("row", "col", None),
            P(),
            P(),
        ),
        out_specs=(P(None, "row", "col"), P()),
        check_vma=False,
    )
```

profile of v0, /device:TPU:1, one launch (start us, length us, event | category | flops | bytes accessed | tf_op | source)
XLA Modules:
  0.0 561.9 jit_solution(17776065899270002200)
XLA Ops:
  7.2 0.9 fusion.65
  8.1 1.4 collective-permute-start.1
  9.5 5.5 collective-permute-start
  15.3 1.0 collective-permute-done
  16.5 4.6 collective-permute-start.2
  21.1 5.1 collective-permute-start.3
  26.3 2.5 collective-permute-done.3
  29.3 0.9 copy-done.1
  30.2 93.5 %while.18 = (s32[]{:T(128)}, f32[3,256,256]{2,1,0:T(8,128)S(1)}, f32[4,3,128,128]{3,2,1,0:T(8,128)S(1)}, s32[]{:T(128)}, s32[1,1,12,2]{2,3,1,0:T(2,128)S(1)}, /*...) while((s32[]{:T(128)}, f32[3,256,256]{2,1,0:T(8,128)S(1)}, ...), condition=%wide.region_1.2_spmd, body=%wide.region_0.1_spmd.sunk | while | flops 69387064 | bytes 8684487 | solution.py:166
  31.5 0.8 fusion.104
  32.2 0.7 constant_dynamic-slice_fusion.5
  37.8 2.6 fusion.106
  41.0 0.8 multiply_convert_fusion.5
  42.6 2.9 dynamic_update_slice.6
  46.9 0.8 fusion.104
  47.6 0.7 constant_dynamic-slice_fusion.5
  53.2 2.6 fusion.106
  56.4 0.8 multiply_convert_fusion.5
  58.0 3.0 dynamic_update_slice.6
  62.4 0.8 fusion.104
  63.2 0.7 constant_dynamic-slice_fusion.5
  68.8 2.6 fusion.106
  71.9 0.8 multiply_convert_fusion.5
  73.5 3.0 dynamic_update_slice.6
  77.9 0.8 fusion.104
  78.7 0.7 constant_dynamic-slice_fusion.5
  84.3 2.6 fusion.106
  87.4 0.8 multiply_convert_fusion.5
  89.0 3.0 dynamic_update_slice.6
  93.4 0.8 fusion.104
  94.2 0.7 constant_dynamic-slice_fusion.5
  99.8 2.6 fusion.106
  102.9 0.8 multiply_convert_fusion.5
  104.5 2.9 dynamic_update_slice.6
  108.9 0.8 fusion.104
  109.7 0.7 constant_dynamic-slice_fusion.5
  115.2 2.6 fusion.106
  118.4 0.8 multiply_convert_fusion.5
  120.0 2.9 dynamic_update_slice.6
  123.8 3.6 collective-permute-start.4
  127.4 1.3 collective-permute-start.5
  128.7 1.2 collective-permute-done.4
  130.0 35.0 %collective-permute-done.5 = f32[3,64,256]{2,1,0:T(8,128)S(1)} collective-permute-done((f32[3,64,256]{2,1,0:T(8,128)S(1)}, f32[3,64,256]{2,1,0:T(8,128)S(1)}, u32[]{:S(2)}, u32[]{:S(2)}) %collective-permute-start.5) | collective-permute-done | bytes 196640 | tf_op jit(solution)/shard_map/ppermute | solution.py:21
  165.1 30.6 %collective-permute-start.6 = (f32[3,128,64]{2,1,0:T(8,128)S(1)}, f32[3,128,64]{2,1,0:T(8,128)S(1)}, u32[]{:S(2)}, u32[]{:S(2)}) collective-permute-start(f32[3,128,64]{2,1,0:T(8,128)S(1)} %get-tuple-element.284), channel_id=1, source_target_pairs={{0,1},{1,2},{2,3},{3,4},{4,5},{5,6},{6,7},{7,8},{8,9},{9,10},{10,1... | collective-permute-start | bytes 294920 | tf_op jit(solution)/shard_map/ppermute | solution.py:18
  195.9 32.5 %collective-permute-start.7 = (f32[3,128,64]{2,1,0:T(8,128)S(1)}, f32[3,128,64]{2,1,0:T(8,128)S(1)}, u32[]{:S(2)}, u32[]{:S(2)}) collective-permute-start(f32[3,128,64]{2,1,0:T(8,128)S(1)} %get-tuple-element.283), channel_id=1, source_target_pairs={{1,0},{2,1},{3,2},{4,3},{5,4},{6,5},{7,6},{8,7},{9,8},{10,9},{11,1... | collective-permute-start | bytes 294920 | tf_op jit(solution)/shard_map/ppermute | solution.py:21
  229.6 1.1 scatter-add.19
  230.6 0.7 fusion.46
  231.3 279.0 %all-reduce.2.cloned.1.call-done = f32[4,3,128,128]{3,2,1,0:T(8,128)} async-done(((f32[4,3,128,128]{3,2,1,0:T(8,128)}), f32[4,3,128,128]{3,2,1,0:T(8,128)}) %all-reduce.2.cloned.1.call-update) | async-done | bytes 786448 | tf_op jit(solution)/shard_map/psum | solution.py:179
  510.3 1.0 fusion.44
  511.3 1.1 fusion.43
  512.8 0.7 add_reduce_fusion.9
  514.6 0.7 add_reduce_fusion.8
  515.3 1.4 maximum_multiply_fusion
  517.4 2.0 add_reduce_fusion.7
  519.9 0.7 add_reduce_fusion.6
  520.6 2.5 maximum_multiply_fusion.1
  523.8 3.1 add_reduce_fusion.4
  527.6 0.7 subtract_reduce_fusion
  528.3 3.8 stack.137
  532.8 4.4 add_reduce_fusion
  537.9 3.8 subtract_multiply_fusion.3
  541.7 6.2 %subtract_multiply_fusion = f32[1,1,128,128]{3,2,1,0:T(8,128)S(1)} fusion(f32[1,1,128,128]{3,2,1,0:T(8,128)S(1)} %get-tuple-element.249, f32[1,1,128,128]{3,2,1,0:T(8,128)S(1)} %get-tuple-element.248, f32[1,1,128,128]{3,2,1,0:T(8,128)S(1)} %bitcast.234, f32[1,1,128,128]{3,2,1,0:T(8,128)S(1)} %bitcast.217, f32[1,1,128,128]{3,2,1,0:T(8,128)S(1)} %bitcast.207, ...), kind=kLoop, calls=%fused_computation.103 | loop fusion | flops 507904 | bytes 524336 | tf_op jit(solution)/shard_map/mul | solution.py:128
  547.9 6.2 %subtract_multiply_fusion.2 = (f32[1,1,128,128]{3,2,1,0:T(8,128)S(1)}, f32[1,1,128,128]{3,2,1,0:T(8,128)S(1)}) fusion(f32[1,1,128,128]{3,2,1,0:T(8,128)S(1)} %get-tuple-element.249, f32[1,1,128,128]{3,2,1,0:T(8,128)S(1)} %get-tuple-element.248, f32[1,1,128,128]{3,2,1,0:T(8,128)S(1)} %bitcast.228, f32[1,1,128,128]{3,2,1,0:T(8,128)S(1)} %bitcast.218, ...), kind=kLoop, calls=%fused_computation.112 | loop fusion | flops 507904 | bytes 589872 | tf_op jit(solution)/shard_map/mul | solution.py:128
  554.2 0.8 maximum_maximum_fusion
  (151 shorter events, 22.2 us)
Async XLA Ops:
  7.2 503.2 %all-reduce.2.cloned.1.call-start = ((), (), s32[]{:S(2)}) async-start(), calls=%async_computation | async-start | bytes 1572864 | tf_op jit(solution)/shard_map/psum | solution.py:179
  8.1 8.2 %copy-start.2 = (f32[2,128,128]{2,1,0:T(8,128)S(1)}, f32[2,128,128]{2,1,0:T(8,128)}, u32[]{:S(2)}) copy-start(f32[2,128,128]{2,1,0:T(8,128)} %param.17) | copy-start | bytes 393220
  8.1 8.2 %collective-permute-start.1 = (f32[2,64,128]{2,1,0:T(8,128)S(1)}, f32[2,64,128]{2,1,0:T(8,128)S(1)}, u32[]{:S(2)}, u32[]{:S(2)}) collective-permute-start(f32[2,64,128]{2,1,0:T(8,128)S(1)} %get-tuple-element.289), channel_id=1, source_target_pairs={{16,0},{32,16},{48,32},{64,48},{80,64},{96,80},{112,96},{128,112},... | collective-permute-start | bytes 196616 | tf_op jit(solution)/shard_map/ppermute | solution.py:21
  9.5 6.8 %collective-permute-start = (f32[2,64,128]{2,1,0:T(8,128)S(1)}, f32[2,64,128]{2,1,0:T(8,128)S(1)}, u32[]{:S(2)}, u32[]{:S(2)}) collective-permute-start(f32[2,64,128]{2,1,0:T(8,128)S(1)} %get-tuple-element.290), channel_id=1, source_target_pairs={{0,16},{16,32},{32,48},{48,64},{64,80},{80,96},{96,112},{112,128},... | collective-permute-start | bytes 196616 | tf_op jit(solution)/shard_map/ppermute | solution.py:18
  16.5 9.8 %collective-permute-start.2 = (f32[2,256,64]{2,1,0:T(8,128)S(1)}, f32[2,256,64]{2,1,0:T(8,128)S(1)}, u32[]{:S(2)}, u32[]{:S(2)}) collective-permute-start(f32[2,256,64]{2,1,0:T(8,128)S(1)} %get-tuple-element.287), channel_id=1, source_target_pairs={{0,1},{1,2},{2,3},{3,4},{4,5},{5,6},{6,7},{7,8},{8,9},{9,10},{10,1... | collective-permute-start | bytes 393224 | tf_op jit(solution)/shard_map/ppermute | solution.py:18
  21.1 7.7 %collective-permute-start.3 = (f32[2,256,64]{2,1,0:T(8,128)S(1)}, f32[2,256,64]{2,1,0:T(8,128)S(1)}, u32[]{:S(2)}, u32[]{:S(2)}) collective-permute-start(f32[2,256,64]{2,1,0:T(8,128)S(1)} %get-tuple-element.288), channel_id=1, source_target_pairs={{1,0},{2,1},{3,2},{4,3},{5,4},{6,5},{7,6},{8,7},{9,8},{10,9},{11,1... | collective-permute-start | bytes 393224 | tf_op jit(solution)/shard_map/ppermute | solution.py:21
  29.2 1.0 copy-start.1
  29.2 1.0 copy-start.3
  29.2 1.0 copy-start.4
  29.2 1.0 copy-start.5
  123.7 3.7 copy-start
  123.8 6.2 %collective-permute-start.4 = (f32[3,64,256]{2,1,0:T(8,128)S(1)}, f32[3,64,256]{2,1,0:T(8,128)S(1)}, u32[]{:S(2)}, u32[]{:S(2)}) collective-permute-start(f32[3,64,256]{2,1,0:T(8,128)S(1)} %get-tuple-element.274), channel_id=1, source_target_pairs={{0,16},{16,32},{32,48},{48,64},{64,80},{80,96},{96,112},{112,128},... | collective-permute-start | bytes 589832 | tf_op jit(solution)/shard_map/ppermute | solution.py:18
  127.4 37.5 %collective-permute-start.5 = (f32[3,64,256]{2,1,0:T(8,128)S(1)}, f32[3,64,256]{2,1,0:T(8,128)S(1)}, u32[]{:S(2)}, u32[]{:S(2)}) collective-permute-start(f32[3,64,256]{2,1,0:T(8,128)S(1)} %get-tuple-element.273), channel_id=1, source_target_pairs={{16,0},{32,16},{48,32},{64,48},{80,64},{96,80},{112,96},{128,112},... | collective-permute-start | bytes 589832 | tf_op jit(solution)/shard_map/ppermute | solution.py:21
  165.1 63.2 %collective-permute-start.6 = (f32[3,128,64]{2,1,0:T(8,128)S(1)}, f32[3,128,64]{2,1,0:T(8,128)S(1)}, u32[]{:S(2)}, u32[]{:S(2)}) collective-permute-start(f32[3,128,64]{2,1,0:T(8,128)S(1)} %get-tuple-element.284), channel_id=1, source_target_pairs={{0,1},{1,2},{2,3},{3,4},{4,5},{5,6},{6,7},{7,8},{8,9},{9,10},{10,1... | collective-permute-start | bytes 294920 | tf_op jit(solution)/shard_map/ppermute | solution.py:18
  195.9 33.5 %collective-permute-start.7 = (f32[3,128,64]{2,1,0:T(8,128)S(1)}, f32[3,128,64]{2,1,0:T(8,128)S(1)}, u32[]{:S(2)}, u32[]{:S(2)}) collective-permute-start(f32[3,128,64]{2,1,0:T(8,128)S(1)} %get-tuple-element.283), channel_id=1, source_target_pairs={{1,0},{2,1},{3,2},{4,3},{5,4},{6,5},{7,6},{8,7},{9,8},{10,9},{11,1... | collective-permute-start | bytes 294920 | tf_op jit(solution)/shard_map/ppermute | solution.py:21
Sparse Core Ops, SparseCore 0:
  195.9 314.4 all-reduce.1
where the time goes:
time: 565 us; the launch traced here: 562 us
  waiting for transfers between devices  319 us (56%)
  starting transfers between devices  84.7 us (15%)
  other arithmetic  63.3 us (11%)
  local copies, waits for them, and re-layouts  39.8 us (7%)
  loops' own time  29.4 us (5%)
  between operations  17 us (3%)
  matrix products  8.53 us (2%)
    psum x1, waiting for transfers between devices, body(): totals = lax.psum(sums, ('row', 'col'))  279 us
    ppermute x4, starting transfers between devices, padded(): lax.ppermute(lax.slice_in_dim(block, block.shape[dim] - width, None, axis...  44.3 us
    ppermute x4, starting transfers between devices, padded(): lax.ppermute(lax.slice_in_dim(block, 0, width, axis=dim), axis, backward)  40.3 us
    ppermute x4, waiting for transfers between devices, padded(): lax.ppermute(lax.slice_in_dim(block, 0, width, axis=dim), axis, backward)  37.9 us
    another operation x1, loops' own time, body(): margins, sums = lax.fori_loop(zero, counts[0, 0], visit, (margins, sums))  29.4 us
    dynamic_update_slice x6, local copies, waits for them, and re-layouts, visit(): lax.dynamic_update_slice(margin_acc, current + object_piece, (zero, top,...  17.6 us
    mul x3, other arithmetic, orthonormal_sequential(): basis.append((vec_real * scale, vec_imag * scale))  16.3 us
    convert_element_type x6, other arithmetic, exit_change(): psi_real.astype(jnp.bfloat16)  15.9 us
  transfers between devices with their start and end apart: 9, of which 6 were waited for; matrix products, arithmetic and copies ran while one was open for 1% of the time, Pallas kernels for 0%

commit v1 on v0

v1 whole, which is shorter than its diff:
```python
import functools

import jax
import jax.numpy as jnp
import ml_dtypes
import numpy as np
from jax import lax
from jax.experimental import pallas as pl
from jax.experimental.pallas import tpu as pltpu
from jax.sharding import PartitionSpec as P

FLOOR = 0.25
RELAX = 0.5
EPSILON = 1e-06
GROUP = 2
MESH = pl.DeviceIdType.MESH
VMEM = pl.BlockSpec(memory_space=pltpu.VMEM)
SMEM = pl.BlockSpec(memory_space=pltpu.SMEM)


def tables(size):
    index = np.arange(size)
    angle = (index[:, None] * index[None, :] % size).astype(np.float32) * np.float32(2.0 * np.pi / size)
    factor = np.float32(1.0 / np.sqrt(size))
    c = (np.cos(angle) * factor).astype(ml_dtypes.bfloat16)
    s = (np.sin(angle) * factor).astype(ml_dtypes.bfloat16)
    p = np.concatenate([np.concatenate([c, s], 1), np.concatenate([-s, c], 1)], 0)
    q = np.concatenate([np.concatenate([c, -s], 1), np.concatenate([s, c], 1)], 0)
    return np.stack([p, q])


def lanes_iota(shape):
    return lax.broadcasted_iota(jnp.int32, shape, len(shape) - 1)


def pack_low(x):
    n = x.shape[1] // 2
    a, b = x[:, :n], x[:, n:]
    return jnp.where(lanes_iota(a.shape) < 64, a, pltpu.roll(b, 64, 2))


def pack_high(x):
    n = x.shape[1] // 2
    a, b = x[:, :n], x[:, n:]
    return jnp.where(lanes_iota(a.shape) < 64, pltpu.roll(a, 64, 2), b)


def unpack_low(x):
    return jnp.concatenate([x, pltpu.roll(x, 64, 2)], 1)


def unpack_high(x):
    return jnp.concatenate([pltpu.roll(x, 64, 2), x], 1)


def place(rows, cols):
    row, col = lax.axis_index("row"), lax.axis_index("col")
    around = {}
    for dr in (-1, 0, 1):
        for dc in (-1, 0, 1):
            if dr or dc:
                around[dr, dc] = (lax.rem(row + dr + rows, rows), lax.rem(col + dc + cols, cols))
    return row, col, around


def inside(row, col, rows, cols, dr, dc):
    ok = jnp.float32(1.0)
    if dr == -1:
        ok = ok * (row > 0).astype(jnp.float32)
    if dr == 1:
        ok = ok * (row < rows - 1).astype(jnp.float32)
    if dc == -1:
        ok = ok * (col > 0).astype(jnp.float32)
    if dc == 1:
        ok = ok * (col < cols - 1).astype(jnp.float32)
    return ok


SIDES = [(-1, 0), (1, 0), (0, -1), (0, 1), (-1, -1), (-1, 1), (1, -1), (1, 1)]


def greet(devices):
    barrier = pltpu.get_barrier_semaphore()
    for device in devices:
        pl.semaphore_signal(barrier, inc=1, device_id=device, device_id_type=MESH)
    pl.semaphore_wait(barrier, len(devices))


def halo_kernel(rows, cols, o_ref, t_ref, ps, pc, rv, rs, rc, send, recv):
    row, col, around = place(rows, cols)
    o = o_ref[...]
    ps[0] = pack_low(o)
    ps[1] = pack_high(o)
    pc[0] = pack_low(o[:, :64])
    pc[1] = pack_high(o[:, :64])
    pc[2] = pack_low(o[:, 64:])
    pc[3] = pack_high(o[:, 64:])
    greet([around[s] for s in SIDES])
    source = {
        (-1, 0): o_ref.at[:, 0:64],
        (1, 0): o_ref.at[:, 64:128],
        (0, -1): ps.at[0],
        (0, 1): ps.at[1],
        (-1, -1): pc.at[0],
        (-1, 1): pc.at[1],
        (1, -1): pc.at[2],
        (1, 1): pc.at[3],
    }
    target = {
        (-1, 0): rv.at[0],
        (1, 0): rv.at[1],
        (0, -1): rs.at[0],
        (0, 1): rs.at[1],
        (-1, -1): rc.at[0],
        (-1, 1): rc.at[1],
        (1, -1): rc.at[2],
        (1, 1): rc.at[3],
    }
    copies = []
    for i, s in enumerate(SIDES):
        copy = pltpu.make_async_remote_copy(
            src_ref=source[s], dst_ref=target[s], send_sem=send.at[i], recv_sem=recv.at[i],
            device_id=around[s], device_id_type=MESH,
        )
        copy.start()
        copies.append(copy)
    t_ref[:, 1, 64:192] = o
    for copy in copies:
        copy.wait()

    def ok(dr, dc):
        return inside(row, col, rows, cols, dr, dc)

    t_ref[:, 1, 192:256] = rv[0] * ok(1, 0)
    t_ref[:, 1, 0:64] = rv[1] * ok(-1, 0)
    t_ref[:, 2, 64:192] = unpack_low(rs[0] * ok(0, 1))
    t_ref[:, 0, 64:192] = unpack_high(rs[1] * ok(0, -1))
    t_ref[:, 2, 192:256] = unpack_low(rc[0] * ok(1, 1))
    t_ref[:, 0, 192:256] = unpack_high(rc[1] * ok(1, -1))
    t_ref[:, 2, 0:64] = unpack_low(rc[2] * ok(-1, 1))
    t_ref[:, 0, 0:64] = unpack_high(rc[3] * ok(-1, -1))


def work_kernel(cap, mixes, counts, offs, index, mix, t_ref, modes, amps, tab, m_ref, s_ref):
    n = 128
    m_ref[...] = jnp.zeros_like(m_ref)
    s_ref[...] = jnp.zeros_like(s_ref)
    count = counts[0, 0]
    fwd, inv = tab[0], tab[1]

    def dot(a, b):
        return jnp.dot(a, b, preferred_element_type=jnp.float32)

    def left(table, res, ims):
        out = dot(table, jnp.concatenate([jnp.concatenate(res, 1), jnp.concatenate(ims, 1)], 0))
        return (
            [out[:n, i * n : (i + 1) * n] for i in range(len(res))],
            [out[n:, i * n : (i + 1) * n] for i in range(len(res))],
        )

    def right(table, res, ims):
        out = dot(jnp.concatenate([jnp.concatenate([a, b], 1) for a, b in zip(res, ims)], 0), table)
        return (
            [out[i * n : (i + 1) * n, :n] for i in range(len(res))],
            [out[i * n : (i + 1) * n, n:] for i in range(len(res))],
        )

    def half(xs):
        return [x.astype(jnp.bfloat16) for x in xs]

    lane = lanes_iota((n, n))

    def visit(step, carry):
        slots = [step * GROUP + i for i in range(GROUP)]
        where, weights, patches, probes, psi = [], [], [], [], []
        for slot in slots:
            top = jnp.clip(offs[0, 0, slot, 0], 0, n - 1)
            left_px = jnp.clip(offs[0, 0, slot, 1], 0, n - 1)
            first = left_px // 64
            shift = lax.rem(left_px + 64, n)
            pick = jnp.clip(index[0, 0, slot], 0, mixes - 1)
            listed = slot < count
            w = [jnp.where(listed, mix[pick, k], 0.0) for k in range(4)]
            mask = lane >= shift
            patch = []
            for comp in range(2):
                a = t_ref[comp, first, pl.ds(top, n), :]
                b = t_ref[comp, first + 1, pl.ds(top, n), :]
                patch.append(pltpu.roll(jnp.where(mask, a, b), lax.rem(n - shift, n), 1))
            probe = []
            for comp in range(2):
                total = w[0] * modes[0, comp]
                for k in range(1, 4):
                    total = total + w[k] * modes[k, comp]
                probe.append(total)
            where.append((top, first, shift, mask))
            weights.append(w)
            patches.append(patch)
            probes.append(probe)
            psi.append(
                (
                    probe[0] * patch[0] - probe[1] * patch[1],
                    probe[0] * patch[1] + probe[1] * patch[0],
                )
            )
        re, im = left(fwd, half([p[0] for p in psi]), half([p[1] for p in psi]))
        re, im = right(inv, half(re), half(im))
        fixed_re, fixed_im = [], []
        for slot, a, b in zip(slots, re, im):
            ratio = amps[0, 0, slot].astype(jnp.float32) * lax.rsqrt(jnp.maximum(a * a + b * b, FLOOR * FLOOR))
            fixed_re.append((a * ratio).astype(jnp.bfloat16))
            fixed_im.append((b * ratio).astype(jnp.bfloat16))
        re, im = left(inv, fixed_re, fixed_im)
        re, im = right(fwd, half(re), half(im))
        pieces = []
        for i in range(GROUP):
            dr, di = re[i] - psi[i][0], im[i] - psi[i][1]
            pr, pi = probes[i]
            ar, ai = patches[i]
            top, first, shift, mask = where[i]
            for f, value in enumerate((pr * dr + pi * di, pr * di - pi * dr, pr * pr + pi * pi)):
                rolled = pltpu.roll(value, shift, 1)
                m_ref[f, first, pl.ds(top, n), :] += jnp.where(mask, rolled, 0.0)
                m_ref[f, first + 1, pl.ds(top, n), :] += jnp.where(mask, 0.0, rolled)
            pieces.append((ar * dr + ai * di, ar * di - ai * dr, ar * ar + ai * ai))
        for k in range(4):
            for f in range(3):
                total = s_ref[k, f]
                for i in range(GROUP):
                    w = weights[i][k]
                    total = total + (w if f < 2 else w * w) * pieces[i][f]
                s_ref[k, f] = total
        return carry

    lax.fori_loop(0, cap // GROUP, visit, 0)


def reduce_kernel(
    rows, cols, nx, n1,
    o_ref, m_ref, s_ref, modes, new_object, new_modes,
    op, oc, orv, ors, orc, got, half, r1, r2, r3, fresh, send, recv,
):
    nz = rows // nx
    row, col, around = place(rows, cols)
    x, z = row // nz, lax.rem(row, nz)
    y, core = col // 2, lax.rem(col, 2)
    p1 = z + core * (y - z)
    p2 = y + core * (z - y)
    sibling = (row, col + 1 - 2 * core)
    high = 2 * core

    def first_peer(a):
        return (x * nz + z + (1 - core) * (a - z), (y + core * (a - y)) * 2 + core)

    def second_peer(a):
        return (x * nz + z + core * (a - z), (y + (1 - core) * (a - y)) * 2 + core)

    def x_peer(a):
        return (a * nz + z, col)

    firsts = [lax.rem(p1 + d, n1) for d in range(1, n1)]
    seconds = [lax.rem(p2 + d, n1) for d in range(1, n1)]
    xs = [lax.rem(x + d, nx) for d in range(1, nx)]
    used = [0]

    def copy(src, dst, device):
        i = used[0]
        used[0] += 1
        made = pltpu.make_async_remote_copy(
            src_ref=src, dst_ref=dst, send_sem=send.at[i], recv_sem=recv.at[i],
            device_id=device, device_id_type=MESH,
        )
        made.start()
        return made

    thick = 128 // n1
    op[0] = pack_high(m_ref[:, 0, 64:192])
    op[1] = pack_low(m_ref[:, 2, 64:192])
    oc[0] = pack_high(m_ref[:, 0, 0:64])
    oc[1] = pack_low(m_ref[:, 2, 0:64])
    oc[2] = pack_high(m_ref[:, 0, 192:256])
    oc[3] = pack_low(m_ref[:, 2, 192:256])
    greet(
        [around[s] for s in SIDES]
        + [sibling]
        + [first_peer(a) for a in firsts]
        + [second_peer(a) for a in seconds]
        + [x_peer(a) for a in xs]
    )
    pending = []
    pair = copy(s_ref.at[pl.ds(2 - high, 2)], got, sibling)
    pair.wait_recv()
    half[...] = s_ref[pl.ds(high, 2)] + got[...]
    pending.append(pair)
    sent = [
        copy(half.at[:, :, pl.ds(pl.multiple_of(a * thick, thick), thick)], r1.at[d], first_peer(a))
        for d, a in enumerate(firsts)
    ]
    edge = [
        copy(m_ref.at[:, 1, 0:64], orv.at[0], around[-1, 0]),
        copy(m_ref.at[:, 1, 192:256], orv.at[1], around[1, 0]),
        copy(op.at[0], ors.at[0], around[0, -1]),
        copy(op.at[1], ors.at[1], around[0, 1]),
        copy(oc.at[0], orc.at[0], around[-1, -1]),
        copy(oc.at[1], orc.at[1], around[-1, 1]),
        copy(oc.at[2], orc.at[2], around[1, -1]),
        copy(oc.at[3], orc.at[3], around[1, 1]),
    ]
    mine = pl.ds(pl.multiple_of(p1 * thick, thick), thick)
    total = half[:, :, mine]
    for d, c in enumerate(sent):
        c.wait_recv()
        total = total + r1[d]
    pending += sent
    tiles = thick // 8
    for m in range(2):
        for t in range(tiles):
            r2[m * tiles + t] = total[m, :, t * 8 : (t + 1) * 8]
    sent = [copy(r2.at[a], r2.at[nx + d], x_peer(a)) for d, a in enumerate(xs)]
    total = r2[x]
    for d, c in enumerate(sent):
        c.wait_recv()
        total = total + r2[nx + d]
    pending += sent
    r3[p2] = total
    sent = [copy(r3.at[p2], r3.at[p2], second_peer(a)) for a in seconds]
    for c in sent:
        c.wait_recv()
    pending += sent
    total = r3[0]
    for a in range(1, n1):
        total = total + r3[a]
    mode, tile = high + x // tiles, lax.rem(x, tiles)
    unit = pl.ds(pl.multiple_of(p1 * thick + tile * 8, 8), 8)
    fresh[mode, :, unit] = modes[mode, :, unit] + total[:2] / (total[2:] + RELAX)
    sent = [copy(fresh.at[mode, :, unit], fresh.at[mode, :, unit], x_peer(a)) for a in xs]
    for c in sent:
        c.wait_recv()
    pending += sent
    both = pl.ds(high, 2)
    sent = [copy(fresh.at[both, :, mine], fresh.at[both, :, mine], first_peer(a)) for a in firsts]

    for c in edge:
        c.wait_recv()
    pending += edge

    def ok(dr, dc):
        return inside(row, col, rows, cols, dr, dc)

    lane = lanes_iota((3, 64, 128))
    west = unpack_low(ors[1] * ok(0, -1))
    east = unpack_high(ors[0] * ok(0, 1))
    for part, vertical, low, top in (
        (slice(0, 64), orv[1] * ok(-1, 0), orc[3] * ok(-1, -1), orc[2] * ok(-1, 1)),
        (slice(64, 128), orv[0] * ok(1, 0), orc[1] * ok(1, -1), orc[0] * ok(1, 1)),
    ):
        sums = m_ref[:, 1, 64 + part.start : 64 + part.stop] + vertical
        side = jnp.where(
            lane < 64, west[:, part] + unpack_low(low), east[:, part] + unpack_high(top)
        )
        sums = sums + side
        new_object[:, part] = o_ref[:, part] + sums[:2] / (sums[2:] + RELAX)

    for c in sent:
        c.wait_recv()
    pending += sent
    pair = copy(fresh.at[both], fresh.at[both], sibling)
    pair.wait_recv()
    pending.append(pair)

    scale = 1.0 / (128 * 128)

    def mean(v):
        return jnp.sum(jnp.sum(v, 0, keepdims=True), 1, keepdims=True) * scale

    basis = []
    coefs = {}
    for k in range(4):
        vr, vi = fresh[k, 0], fresh[k, 1]
        for j in range(k):
            cr, ci = coefs[j, k]
            br, bi = basis[j]
            vr = vr - (cr * br - ci * bi)
            vi = vi - (cr * bi + ci * br)
        norm = 1.0 / jnp.sqrt(mean(vr * vr + vi * vi) + EPSILON)
        qr, qi = vr * norm, vi * norm
        basis.append((qr, qi))
        new_modes[k, 0] = qr
        new_modes[k, 1] = qi
        for later in range(k + 1, 4):
            fr, fi = fresh[later, 0], fresh[later, 1]
            coefs[k, later] = (mean(qr * fr + qi * fi), mean(qr * fi - qi * fr))
    for c in pending:
        c.wait_send()


def halo(rows, cols, object_field):
    f32 = jnp.float32
    return pl.pallas_call(
        functools.partial(halo_kernel, rows, cols),
        out_shape=jax.ShapeDtypeStruct((2, 3, 256, 128), f32),
        in_specs=[VMEM],
        out_specs=VMEM,
        scratch_shapes=[
            pltpu.VMEM((2, 2, 64, 128), f32),
            pltpu.VMEM((4, 2, 32, 128), f32),
            pltpu.VMEM((2, 2, 64, 128), f32),
            pltpu.VMEM((2, 2, 64, 128), f32),
            pltpu.VMEM((4, 2, 32, 128), f32),
            pltpu.SemaphoreType.DMA((8,)),
            pltpu.SemaphoreType.DMA((8,)),
        ],
        compiler_params=pltpu.CompilerParams(collective_id=0, has_side_effects=True),
        name="halo",
    )(object_field)


def work(counts, offsets, mode_index, mix_table, tiles, probe_modes, amplitudes):
    f32 = jnp.float32
    return pl.pallas_call(
        functools.partial(work_kernel, amplitudes.shape[2], mix_table.shape[0]),
        out_shape=(
            jax.ShapeDtypeStruct((3, 3, 256, 128), f32),
            jax.ShapeDtypeStruct((4, 3, 128, 128), f32),
        ),
        in_specs=[SMEM] * 4 + [VMEM] * 4,
        out_specs=(VMEM, VMEM),
        compiler_params=pltpu.CompilerParams(vmem_limit_bytes=48 * 1024 * 1024),
        name="work",
    )(counts, offsets, mode_index, mix_table, tiles, probe_modes, amplitudes, jnp.asarray(tables(128)))


def reduce(rows, cols, nx, object_field, margins, sums, probe_modes):
    f32 = jnp.float32
    n1 = cols // 2
    count = 8 + 2 + 4 * (n1 - 1) + 2 * (nx - 1)
    return pl.pallas_call(
        functools.partial(reduce_kernel, rows, cols, nx, n1),
        out_shape=(
            jax.ShapeDtypeStruct((2, 128, 128), f32),
            jax.ShapeDtypeStruct((4, 2, 128, 128), f32),
        ),
        in_specs=[VMEM] * 4,
        out_specs=(VMEM, VMEM),
        scratch_shapes=[
            pltpu.VMEM((2, 3, 64, 128), f32),
            pltpu.VMEM((4, 3, 32, 128), f32),
            pltpu.VMEM((2, 3, 64, 128), f32),
            pltpu.VMEM((2, 3, 64, 128), f32),
            pltpu.VMEM((4, 3, 32, 128), f32),
            pltpu.VMEM((2, 3, 128, 128), f32),
            pltpu.VMEM((2, 3, 128, 128), f32),
            pltpu.VMEM((n1 - 1, 2, 3, 128 // n1, 128), f32),
            pltpu.VMEM((2 * nx, 3, 8, 128), f32),
            pltpu.VMEM((n1, 3, 8, 128), f32),
            pltpu.VMEM((4, 2, 128, 128), f32),
            pltpu.SemaphoreType.DMA((count,)),
            pltpu.SemaphoreType.DMA((count,)),
        ],
        compiler_params=pltpu.CompilerParams(
            collective_id=1, has_side_effects=True, vmem_limit_bytes=48 * 1024 * 1024
        ),
        name="reduce",
    )(object_field, margins, sums, probe_modes)


def solution(mesh):
    rows, cols = mesh.shape["row"], mesh.shape["col"]
    nx = 4

    def body(object_field, amplitudes, counts, offsets, mode_index, mix_table, probe_modes):
        tiles = halo(rows, cols, object_field)
        margins, sums = work(counts, offsets, mode_index, mix_table, tiles, probe_modes, amplitudes)
        return reduce(rows, cols, nx, object_field, margins, sums, probe_modes)

    return jax.shard_map(
        body,
        mesh=mesh,
        in_specs=(
            P(None, "row", "col"),
            P("row", "col", None, None, None),
            P("row", "col"),
            P("row", "col", None, None),
            P("row", "col", None),
            P(),
            P(),
        ),
        out_specs=(P(None, "row", "col"), P()),
        check_vma=False,
    )
```

time: 565 us -> 78.2 us (0.14)
  waiting for transfers between devices: 319 us -> 0 us
  starting transfers between devices: 84.7 us -> 0 us
  Pallas kernels: 0 us -> 70.7 us
  other arithmetic: 63.3 us -> 0 us
  local copies, waits for them, and re-layouts: 39.8 us -> 5.72 us
  loops' own time: 29.4 us -> 0 us
  between operations: 17 us -> 1.43 us
  matrix products: 8.53 us -> 0 us
    psum x1 -> x0, waiting for transfers between devices: 279 us -> none  [body(): totals = lax.psum(sums, ('row', 'col'))]
    ppermute x8 -> x0, starting transfers between devices: 84.6 us -> none  [the longest x4 44.3 us: padded(): lax.ppermute(lax.slice_in_dim(block, block.shape[dim] - width, None, axis...]
    pallas_call x0 -> x3, Pallas kernels: none -> 70.7 us  [the longest x1 42.2 us: reduce(): pl.pallas_call(functools.partial(reduce_kernel, rows, cols, nx, n1), out_...]
    ppermute x8 -> x0, waiting for transfers between devices: 40.2 us -> none  [the longest x4 37.9 us: padded(): lax.ppermute(lax.slice_in_dim(block, 0, width, axis=dim), axis, backward)]
    another operation x1 -> x0, loops' own time: 29.4 us -> none  [body(): margins, sums = lax.fori_loop(zero, counts[0, 0], visit, (margins, sums))]
    convert_element_type x31 -> x0, other arithmetic: 22 us -> none  [the longest x6 15.9 us: exit_change(): psi_real.astype(jnp.bfloat16)]
    dynamic_update_slice x6 -> x0, local copies, waits for them, and re-layouts: 17.6 us -> none  [visit(): lax.dynamic_update_slice(margin_acc, current + object_piece, (zero, top,...]
    mul x3 -> x0, other arithmetic: 16.3 us -> none  [orthonormal_sequential(): basis.append((vec_real * scale, vec_imag * scale))]
  transfers between devices with their start and end apart: 9 -> 0, of which waited for: 6 -> 0; matrix products, arithmetic and copies ran while one was open for 1% -> 0% of each run, Pallas kernels for 0% -> 0%
where the time goes in v1:
time: 78.2 us; the launch traced here: 77.9 us
  Pallas kernels  70.7 us (90%)
  local copies, waits for them, and re-layouts  5.72 us (7%)
  between operations  1.43 us (2%)
    pallas_call x1, Pallas kernels, reduce(): pl.pallas_call(functools.partial(reduce_kernel, rows, cols, nx, n1), out_...  42.2 us
    pallas_call x1, Pallas kernels, halo(): pl.pallas_call(functools.partial(halo_kernel, rows, cols), out_shape=jax....  21.1 us
    pallas_call x1, Pallas kernels, work(): pl.pallas_call(functools.partial(work_kernel, amplitudes.shape[2], mix_ta...  7.5 us
    unnamed x16, local copies, waits for them, and re-layouts  5.72 us

profile of v1, /device:TPU:1, one launch (start us, length us, event | category | flops | bytes accessed | tf_op | source)
XLA Modules:
  0.0 77.9 jit_solution(8237215711760455086)
XLA Ops:
  0.6 0.0 copy-start.1
  0.6 0.0 copy-start.3
  1.4 0.8 copy.10.offs
  2.1 0.8 copy.11.mix
  2.9 21.1 %halo.1.t_ref = f32[2,3,256,128]{3,2,1,0:T(8,128)} custom-call(f32[2,128,128]{2,1,0:T(8,128)} %o_ref.3), custom_call_target="tpu_custom_call" | custom-call | tf_op jit(solution)/shard_map/halo/pallas_call | solution.py:399
  24.0 0.0 copy-done.1
  24.0 0.0 copy-done.3
  24.0 0.0 copy-start
  24.0 1.1 %copy-done = f32[2,3,256,128]{3,2,1,0:T(8,128)S(1)} copy-done((f32[2,3,256,128]{3,2,1,0:T(8,128)S(1)}, f32[2,3,256,128]{3,2,1,0:T(8,128)}, u32[]{:S(2)}) %copy-start) | copy-done | bytes 786456
  25.1 0.0 copy-start.4
  25.1 0.9 %copy-done.4 = bf16[2,256,256]{2,1,0:T(8,128)(2,1)S(1)} copy-done((bf16[2,256,256]{2,1,0:T(8,128)(2,1)S(1)}, bf16[2,256,256]{2,1,0:T(8,128)(2,1)}, u32[]{:S(2)}) %copy-start.4) | copy-done | bytes 262168
  26.1 0.0 copy-start.5
  26.1 0.7 copy-done.5
  26.7 0.0 copy-start.2
  26.7 7.5 %work.1 = (f32[3,3,256,128]{3,2,1,0:T(8,128)S(1)}, f32[4,3,128,128]{3,2,1,0:T(8,128)S(1)}) custom-call(s32[1,1]{1,0:T(1,128)S(6)} %copy.14.counts, s32[1,1,12,2]{3,2,1,0:T(8,128)S(1)} %copy.10.offs, s32[1,1,12]{2,1,0:T(1,128)S(1)} %copy-done.5, f32[16,4]{1,0:T(8,128)S(1)} %copy.11.mix, f32[2,3,256,128]{3,2,1,0:T(8,128)S(1)} %copy-done, ...), custom_call_target="tpu_custom_call" | custom-call | tf_op jit(solution)/shard_map/work/pallas_call | solution.py:420
  34.2 0.0 copy-done.2
  34.3 42.2 %reduce.1 = (f32[2,128,128]{2,1,0:T(8,128)S(1)}, f32[4,2,128,128]{3,2,1,0:T(8,128)S(1)}) custom-call(f32[2,128,128]{2,1,0:T(8,128)S(1)} %copy-done.2, f32[3,3,256,128]{3,2,1,0:T(8,128)S(1)} %get-tuple-element.4.m_ref, f32[4,3,128,128]{3,2,1,0:T(8,128)S(1)} %get-tuple-element.5.s_ref, f32[4,2,128,128]{3,2,1,0:T(8,128)S(1)} %copy-done.1), custom_call_target="tpu_custom_call" | custom-call | tf_op jit(solution)/shard_map/reduce/pallas_call | solution.py:437
  76.4 0.7 copy.15
  77.1 0.8 %copy.16 = f32[4,2,128,128]{3,2,1,0:T(8,128)} copy(f32[4,2,128,128]{3,2,1,0:T(8,128)S(1)} %get-tuple-element.9) | data formatting | bytes 1048576
Async XLA Ops:
  0.6 23.3 %copy-start.1 = (f32[4,2,128,128]{3,2,1,0:T(8,128)S(1)}, f32[4,2,128,128]{3,2,1,0:T(8,128)}, u32[]{:S(2)}) copy-start(f32[4,2,128,128]{3,2,1,0:T(8,128)} %modes.3) | copy-start | bytes 1572868
  0.6 23.3 %copy-start.3 = (bf16[1,1,12,128,128]{4,3,2,1,0:T(8,128)(2,1)S(1)}, bf16[1,1,12,128,128]{4,3,2,1,0:T(8,128)(2,1)}, u32[]{:S(2)}) copy-start(bf16[1,1,12,128,128]{4,3,2,1,0:T(8,128)(2,1)} %amps.1) | copy-start | bytes 1179652
  24.0 1.1 %copy-start = (f32[2,3,256,128]{3,2,1,0:T(8,128)S(1)}, f32[2,3,256,128]{3,2,1,0:T(8,128)}, u32[]{:S(2)}) copy-start(f32[2,3,256,128]{3,2,1,0:T(8,128)} %halo.1.t_ref) | copy-start | bytes 2359300
  25.1 0.9 %copy-start.4 = (bf16[2,256,256]{2,1,0:T(8,128)(2,1)S(1)}, bf16[2,256,256]{2,1,0:T(8,128)(2,1)}, u32[]{:S(2)}) copy-start(bf16[2,256,256]{2,1,0:T(8,128)(2,1)} %constant.2.clone.tab) | copy-start | bytes 786436
  26.1 0.7 copy-start.5
  26.7 7.5 %copy-start.2 = (f32[2,128,128]{2,1,0:T(8,128)S(1)}, f32[2,128,128]{2,1,0:T(8,128)}, u32[]{:S(2)}) copy-start(f32[2,128,128]{2,1,0:T(8,128)} %o_ref.3) | copy-start | bytes 393220

commit v2 on v1

v2 whole, which is shorter than its diff:
```python
import functools

import jax
import jax.numpy as jnp
import ml_dtypes
import numpy as np
from jax import lax
from jax.experimental import pallas as pl
from jax.experimental.pallas import tpu as pltpu
from jax.sharding import PartitionSpec as P

FLOOR = 0.25
RELAX = 0.5
EPSILON = 1e-06
GROUP = 2
FAR = (4, 3, 5, 2, 6, 1, 7)
NEAR = (1, 7, 2, 6, 3, 5, 4)
MESH = pl.DeviceIdType.MESH
VMEM = pl.BlockSpec(memory_space=pltpu.VMEM)
HBM = pl.BlockSpec(memory_space=pltpu.HBM)


def tables(size):
    index = np.arange(size)
    angle = (index[:, None] * index[None, :] % size).astype(np.float32) * np.float32(2.0 * np.pi / size)
    factor = np.float32(1.0 / np.sqrt(size))
    c = (np.cos(angle) * factor).astype(ml_dtypes.bfloat16)
    s = (np.sin(angle) * factor).astype(ml_dtypes.bfloat16)
    p = np.concatenate([np.concatenate([c, s], 1), np.concatenate([-s, c], 1)], 0)
    q = np.concatenate([np.concatenate([c, -s], 1), np.concatenate([s, c], 1)], 0)
    return np.stack([p, q])


def lanes_iota(shape):
    return lax.broadcasted_iota(jnp.int32, shape, len(shape) - 1)


def pack_low(x):
    n = x.shape[1] // 2
    a, b = x[:, :n], x[:, n:]
    return jnp.where(lanes_iota(a.shape) < 64, a, pltpu.roll(b, 64, 2))


def pack_high(x):
    n = x.shape[1] // 2
    a, b = x[:, :n], x[:, n:]
    return jnp.where(lanes_iota(a.shape) < 64, pltpu.roll(a, 64, 2), b)


def unpack_low(x):
    return jnp.concatenate([x, pltpu.roll(x, 64, 2)], 1)


def unpack_high(x):
    return jnp.concatenate([pltpu.roll(x, 64, 2), x], 1)


def place(rows, cols):
    row, col = lax.axis_index("row"), lax.axis_index("col")
    around = {}
    for dr in (-1, 0, 1):
        for dc in (-1, 0, 1):
            if dr or dc:
                around[dr, dc] = (lax.rem(row + dr + rows, rows), lax.rem(col + dc + cols, cols))
    return row, col, around


def inside(row, col, rows, cols, dr, dc):
    ok = jnp.float32(1.0)
    if dr == -1:
        ok = ok * (row > 0).astype(jnp.float32)
    if dr == 1:
        ok = ok * (row < rows - 1).astype(jnp.float32)
    if dc == -1:
        ok = ok * (col > 0).astype(jnp.float32)
    if dc == 1:
        ok = ok * (col < cols - 1).astype(jnp.float32)
    return ok


SIDES = [(-1, 0), (1, 0), (0, -1), (0, 1), (-1, -1), (-1, 1), (1, -1), (1, 1)]


def kernel(
    rows, cols, nx, n1, cap, mixes,
    o_hbm, a_hbm, counts_hbm, offs_hbm, index_hbm, mix_hbm, modes_hbm, tab_hbm,
    new_object, new_modes,
    obj, amps, counts, offs, index, mix, modes, tab,
    ps, pc, rv, rs, rc, tiles, probes, patches, deltas, sums, pad, marg,
    on, op, oc, orv, ors, orc, got, half, r1, r2, r3, fresh,
    load, send, recv,
):
    n = 128
    nz = rows // nx
    row, col, around = place(rows, cols)
    x, z = row // nz, lax.rem(row, nz)
    y, core = col // 2, lax.rem(col, 2)
    p1 = z + core * (y - z)
    p2 = y + core * (z - y)
    sibling = (row, col + 1 - 2 * core)
    high = 2 * core
    other = 2 - high

    def first_peer(d):
        a = lax.rem(p1 + d, n1)
        return a, (x * nz + z + (1 - core) * (a - z), (y + core * (a - y)) * 2 + core)

    def second_peer(d):
        a = lax.rem(p2 + d, n1)
        return a, (x * nz + z + core * (a - z), (y + (1 - core) * (a - y)) * 2 + core)

    def x_peer(d):
        a = lax.rem(x + d, nx)
        return a, (a * nz + z, col)

    used = [0]
    pending = []

    def copy(src, dst, device):
        i = used[0]
        used[0] += 1
        made = pltpu.make_async_remote_copy(
            src_ref=src, dst_ref=dst, send_sem=send.at[i], recv_sem=recv.at[i],
            device_id=device, device_id_type=MESH,
        )
        made.start()
        pending.append(made)
        return made

    def ok(dr, dc):
        return inside(row, col, rows, cols, dr, dc)

    barrier = pltpu.get_barrier_semaphore()
    partners = (
        [around[s] for s in SIDES]
        + [sibling]
        + [first_peer(d)[1] for d in range(1, n1)]
        + [second_peer(d)[1] for d in range(1, n1)]
        + [x_peer(d)[1] for d in range(1, nx)]
    )
    for device in partners:
        pl.semaphore_signal(barrier, inc=1, device_id=device, device_id_type=MESH)
    loads = [
        pltpu.make_async_copy(src, dst, load.at[i])
        for i, (src, dst) in enumerate(
            (
                (o_hbm, obj), (modes_hbm, modes), (mix_hbm, mix), (index_hbm, index), (counts_hbm, counts),
                (offs_hbm, offs), (tab_hbm, tab), (a_hbm, amps),
            )
        )
    ]
    for c in loads:
        c.start()

    loads[0].wait()
    ps[0] = pack_low(obj[...])
    ps[1] = pack_high(obj[...])
    pc[0] = pack_low(obj[:, :64])
    pc[1] = pack_high(obj[:, :64])
    pc[2] = pack_low(obj[:, 64:])
    pc[3] = pack_high(obj[:, 64:])
    pl.semaphore_wait(barrier, len(partners))
    halo = [
        copy(pc.at[0], rc.at[0], around[-1, -1]),
        copy(pc.at[1], rc.at[1], around[-1, 1]),
        copy(pc.at[2], rc.at[2], around[1, -1]),
        copy(pc.at[3], rc.at[3], around[1, 1]),
        copy(obj.at[:, 0:64], rv.at[0], around[-1, 0]),
        copy(obj.at[:, 64:128], rv.at[1], around[1, 0]),
        copy(ps.at[0], rs.at[0], around[0, -1]),
        copy(ps.at[1], rs.at[1], around[0, 1]),
    ]

    for c in loads[1:]:
        c.wait()
    marg[...] = jnp.zeros_like(marg)
    sums[...] = jnp.zeros_like(sums)
    pad[...] = jnp.zeros_like(pad)
    count = counts[0, 0]

    def spot(slot):
        top = jnp.clip(offs[0, 0, 0, slot], 0, n - 1)
        left_px = jnp.clip(offs[0, 0, 1, slot], 0, n - 1)
        return top, left_px

    def weights_of(slot):
        pick = jnp.clip(index[0, 0, slot], 0, mixes - 1)
        return [jnp.where(slot < count, mix[k, pick], 0.0) for k in range(4)]

    def make_probe(slot, carry):
        w = weights_of(slot)
        for comp in range(2):
            total = w[0] * modes[0, comp]
            for k in range(1, 4):
                total = total + w[k] * modes[k, comp]
            probes[slot, comp] = total
        return carry

    lax.fori_loop(0, cap, make_probe, 0)
    for c in halo:
        c.wait_recv()

    def tile_rows(target, west, own, east):
        turned = pltpu.roll(own, 64, 2)
        low = lanes_iota(own.shape) < 64
        tiles[:, 0, target] = jnp.where(low, west, turned)
        tiles[:, 1, target] = jnp.where(low, turned, east)

    tile_rows(
        slice(0, 64), unpack_low(rc[3] * ok(-1, -1)), rv[1] * ok(-1, 0), unpack_high(rc[2] * ok(-1, 1))
    )
    tile_rows(slice(64, 192), unpack_low(rs[1] * ok(0, -1)), obj[...], unpack_high(rs[0] * ok(0, 1)))
    tile_rows(
        slice(192, 256), unpack_low(rc[1] * ok(1, -1)), rv[0] * ok(1, 0), unpack_high(rc[0] * ok(1, 1))
    )

    fwd, inv = tab[0], tab[1]

    def dot(a, b):
        return jnp.dot(a, b, preferred_element_type=jnp.float32)

    def left(table, res, ims):
        out = dot(table, jnp.concatenate([jnp.concatenate(res, 1), jnp.concatenate(ims, 1)], 0))
        return (
            [out[:n, i * n : (i + 1) * n] for i in range(len(res))],
            [out[n:, i * n : (i + 1) * n] for i in range(len(res))],
        )

    def right(table, res, ims):
        out = dot(jnp.concatenate([jnp.concatenate([a, b], 1) for a, b in zip(res, ims)], 0), table)
        return (
            [out[i * n : (i + 1) * n, :n] for i in range(len(res))],
            [out[i * n : (i + 1) * n, n:] for i in range(len(res))],
        )

    def lower(xs):
        return [v.astype(jnp.bfloat16) for v in xs]

    lane = lanes_iota((n, n))

    def visit(step, carry):
        slots = [step * GROUP + i for i in range(GROUP)]
        psi_r, psi_i = [], []
        for slot in slots:
            top, left_px = spot(slot)
            mask = lane >= left_px
            patch = []
            for comp in range(2):
                a = tiles[comp, 0, pl.ds(top, n), :]
                b = tiles[comp, 1, pl.ds(top, n), :]
                patch.append(pltpu.roll(jnp.where(mask, a, b), lax.rem(n - left_px, n), 1))
                patches[slot, comp] = patch[comp]
            pr, pi = probes[slot, 0], probes[slot, 1]
            psi_r.append(pr * patch[0] - pi * patch[1])
            psi_i.append(pr * patch[1] + pi * patch[0])
        re, im = left(fwd, lower(psi_r), lower(psi_i))
        re, im = right(inv, lower(re), lower(im))
        fixed_re, fixed_im = [], []
        for slot, a, b in zip(slots, re, im):
            ratio = amps[0, 0, slot].astype(jnp.float32) * lax.rsqrt(jnp.maximum(a * a + b * b, FLOOR * FLOOR))
            fixed_re.append((a * ratio).astype(jnp.bfloat16))
            fixed_im.append((b * ratio).astype(jnp.bfloat16))
        re, im = left(inv, fixed_re, fixed_im)
        re, im = right(fwd, lower(re), lower(im))
        pieces, weights = [], []
        for i, slot in enumerate(slots):
            dr, di = re[i] - psi_r[i], im[i] - psi_i[i]
            deltas[slot, 0] = dr
            deltas[slot, 1] = di
            ar, ai = patches[slot, 0], patches[slot, 1]
            pieces.append((ar * dr + ai * di, ar * di - ai * dr, ar * ar + ai * ai))
            weights.append(weights_of(slot))
        for k in range(4):
            for f in range(3):
                total = sums[k, f]
                for i in range(GROUP):
                    w = weights[i][k]
                    total = total + (w if f < 2 else w * w) * pieces[i][f]
                sums[k, f] = total
        return carry

    lax.fori_loop(0, cap // GROUP, visit, 0)

    thick = n // n1

    def chunk(a):
        return pl.ds(pl.multiple_of(a * thick, thick), thick)

    order = FAR + (0,)
    pair = []
    for d in order:
        piece = chunk(lax.rem(p2 + d, n1))
        pair.append(copy(sums.at[pl.ds(other, 2), :, piece], got.at[:, :, piece], sibling))
    sent = []
    for d, c in zip(order, pair):
        c.wait_recv()
        a, device = first_peer(d)
        half[:, :, chunk(a)] = sums[pl.ds(high, 2), :, chunk(a)] + got[:, :, chunk(a)]
        if d:
            sent.append(copy(half.at[:, :, chunk(a)], r1.at[d - 1], device))

    def spread(step, carry):
        slots = [step * GROUP + i for i in range(GROUP)]
        spots = [spot(slot) for slot in slots]
        for i, slot in enumerate(slots):
            pr, pi = probes[slot, 0], probes[slot, 1]
            dr, di = deltas[slot, 0], deltas[slot, 1]
            for f, value in enumerate((pr * dr + pi * di, pr * di - pi * dr, pr * pr + pi * pi)):
                pad[i, f, n : 2 * n] = pltpu.roll(value, spots[i][1], 1)
        for f in range(3):
            for h in range(4):
                part = slice(h * 64, (h + 1) * 64)
                low, up = marg[f, 0, part], marg[f, 1, part]
                for i, (top, left_px) in enumerate(spots):
                    value = pad[i, f, pl.ds(n - top + h * 64, 64), :]
                    mask = lanes_iota((64, n)) >= left_px
                    low = low + jnp.where(mask, value, 0.0)
                    up = up + jnp.where(mask, 0.0, value)
                marg[f, 0, part] = low
                marg[f, 1, part] = up
        return carry

    lax.fori_loop(0, cap // GROUP, spread, 0)
    low64 = lanes_iota((3, 64, n)) < 64

    def centre(part):
        return jnp.where(low64, pltpu.roll(marg[:, 0, part], 64, 2), pltpu.roll(marg[:, 1, part], 64, 2))

    on[0] = centre(slice(0, 64))
    on[1] = centre(slice(192, 256))
    op[0] = pack_low(marg[:, 0, 64:192])
    op[1] = pack_high(marg[:, 1, 64:192])
    oc[0] = pack_low(marg[:, 0, 0:64])
    oc[1] = pack_high(marg[:, 1, 0:64])
    oc[2] = pack_low(marg[:, 0, 192:256])
    oc[3] = pack_high(marg[:, 1, 192:256])

    mine = chunk(p1)
    total = half[:, :, mine]
    for d, c in zip(FAR[::-1], sent[::-1]):
        c.wait_recv()
        total = total + r1[d - 1]
    parts = thick // 8
    for m in range(2):
        for t in range(parts):
            r2[m * parts + t] = total[m, :, t * 8 : (t + 1) * 8]
    sent = []
    for d in range(1, nx):
        a, device = x_peer(d)
        sent.append(copy(r2.at[a], r2.at[nx + d - 1], device))
    edge = [
        copy(oc.at[0], orc.at[0], around[-1, -1]),
        copy(oc.at[1], orc.at[1], around[-1, 1]),
        copy(oc.at[2], orc.at[2], around[1, -1]),
        copy(oc.at[3], orc.at[3], around[1, 1]),
        copy(on.at[0], orv.at[0], around[-1, 0]),
        copy(on.at[1], orv.at[1], around[1, 0]),
        copy(op.at[0], ors.at[0], around[0, -1]),
        copy(op.at[1], ors.at[1], around[0, 1]),
    ]
    total = r2[x]
    for d, c in enumerate(sent):
        c.wait_recv()
        total = total + r2[nx + d]
    r3[p2] = total
    sent = []
    for d in FAR:
        _, device = second_peer(d)
        sent.append(copy(r3.at[p2], r3.at[p2], device))
    for c in sent:
        c.wait_recv()
    total = r3[0]
    for a in range(1, n1):
        total = total + r3[a]
    mode, tile = high + x // parts, lax.rem(x, parts)
    unit = pl.ds(pl.multiple_of(p1 * thick + tile * 8, 8), 8)
    fresh[mode, :, unit] = modes[mode, :, unit] + total[:2] / (total[2:] + RELAX)
    sent = []
    for d in range(1, nx):
        _, device = x_peer(d)
        sent.append(copy(fresh.at[mode, :, unit], fresh.at[mode, :, unit], device))
    for c in sent:
        c.wait_recv()
    both = pl.ds(high, 2)
    sent = {}
    for d in FAR:
        _, device = first_peer(d)
        sent[d] = copy(fresh.at[both, :, mine], fresh.at[both, :, mine], device)
    pair = [copy(fresh.at[both, :, mine], fresh.at[both, :, mine], sibling)]

    for c in edge:
        c.wait_recv()
    west = unpack_low(ors[1] * ok(0, -1))
    east = unpack_high(ors[0] * ok(0, 1))
    for part, inner, vertical, lo, up in (
        (slice(0, 64), slice(64, 128), orv[1] * ok(-1, 0), orc[3] * ok(-1, -1), orc[2] * ok(-1, 1)),
        (slice(64, 128), slice(128, 192), orv[0] * ok(1, 0), orc[1] * ok(1, -1), orc[0] * ok(1, 1)),
    ):
        side = jnp.where(low64, west[:, part] + unpack_low(lo), east[:, part] + unpack_high(up))
        both_sums = centre(inner) + vertical + side
        new_object[:, part] = obj[:, part] + both_sums[:2] / (both_sums[2:] + RELAX)

    for d in NEAR:
        sent[d].wait_recv()
        piece = chunk(lax.rem(p1 + n1 - d, n1))
        pair.append(copy(fresh.at[both, :, piece], fresh.at[both, :, piece], sibling))
    for c in pair:
        c.wait_recv()

    scale = 1.0 / (n * n)

    def mean(v):
        return jnp.sum(jnp.sum(v, 0, keepdims=True), 1, keepdims=True) * scale

    basis = []
    coefs = {}
    for k in range(4):
        vr, vi = fresh[k, 0], fresh[k, 1]
        for j in range(k):
            cr, ci = coefs[j, k]
            br, bi = basis[j]
            vr = vr - (cr * br - ci * bi)
            vi = vi - (cr * bi + ci * br)
        norm = 1.0 / jnp.sqrt(mean(vr * vr + vi * vi) + EPSILON)
        qr, qi = vr * norm, vi * norm
        basis.append((qr, qi))
        new_modes[k, 0] = qr
        new_modes[k, 1] = qi
        for later in range(k + 1, 4):
            fr, fi = fresh[later, 0], fresh[later, 1]
            coefs[k, later] = (mean(qr * fr + qi * fi), mean(qr * fi - qi * fr))
    for c in pending:
        c.wait_send()


def solution(mesh):
    rows, cols = mesh.shape["row"], mesh.shape["col"]
    nx = 4
    n1 = cols // 2
    f32, bf16, i32 = jnp.float32, jnp.bfloat16, jnp.int32

    def body(object_field, amplitudes, counts, offsets, mode_index, mix_table, probe_modes):
        cap, mixes = amplitudes.shape[2], mix_table.shape[0]
        number = 16 + 8 + 8 + 3 * (n1 - 1) + 2 * (nx - 1)
        return pl.pallas_call(
            functools.partial(kernel, rows, cols, nx, n1, cap, mixes),
            out_shape=(
                jax.ShapeDtypeStruct((2, 128, 128), f32),
                jax.ShapeDtypeStruct((4, 2, 128, 128), f32),
            ),
            in_specs=[HBM] * 8,
            out_specs=(VMEM, VMEM),
            scratch_shapes=[
                pltpu.VMEM((2, 128, 128), f32),
                pltpu.VMEM(amplitudes.shape, bf16),
                pltpu.SMEM((1, 1), i32),
                pltpu.SMEM((1, 1, 2, cap), i32),
                pltpu.SMEM((1, 1, cap), i32),
                pltpu.SMEM((4, mixes), f32),
                pltpu.VMEM((4, 2, 128, 128), f32),
                pltpu.VMEM((2, 256, 256), bf16),
                pltpu.VMEM((2, 2, 64, 128), f32),
                pltpu.VMEM((4, 2, 32, 128), f32),
                pltpu.VMEM((2, 2, 64, 128), f32),
                pltpu.VMEM((2, 2, 64, 128), f32),
                pltpu.VMEM((4, 2, 32, 128), f32),
                pltpu.VMEM((2, 2, 256, 128), f32),
                pltpu.VMEM((cap, 2, 128, 128), f32),
                pltpu.VMEM((cap, 2, 128, 128), f32),
                pltpu.VMEM((cap, 2, 128, 128), f32),
                pltpu.VMEM((4, 3, 128, 128), f32),
                pltpu.VMEM((GROUP, 3, 384, 128), f32),
                pltpu.VMEM((3, 2, 256, 128), f32),
                pltpu.VMEM((2, 3, 64, 128), f32),
                pltpu.VMEM((2, 3, 64, 128), f32),
                pltpu.VMEM((4, 3, 32, 128), f32),
                pltpu.VMEM((2, 3, 64, 128), f32),
                pltpu.VMEM((2, 3, 64, 128), f32),
                pltpu.VMEM((4, 3, 32, 128), f32),
                pltpu.VMEM((2, 3, 128, 128), f32),
                pltpu.VMEM((2, 3, 128, 128), f32),
                pltpu.VMEM((n1 - 1, 2, 3, 128 // n1, 128), f32),
                pltpu.VMEM((2 * nx, 3, 8, 128), f32),
                pltpu.VMEM((n1, 3, 8, 128), f32),
                pltpu.VMEM((4, 2, 128, 128), f32),
                pltpu.SemaphoreType.DMA((8,)),
                pltpu.SemaphoreType.DMA((number,)),
                pltpu.SemaphoreType.DMA((number,)),
            ],
            compiler_params=pltpu.CompilerParams(
                collective_id=0, has_side_effects=True, vmem_limit_bytes=56 * 1024 * 1024
            ),
            name="update",
        )(
            object_field, amplitudes, counts, jnp.swapaxes(offsets, 2, 3), mode_index, mix_table.T,
            probe_modes, jnp.asarray(tables(128)),
        )

    return jax.shard_map(
        body,
        mesh=mesh,
        in_specs=(
            P(None, "row", "col"),
            P("row", "col", None, None, None),
            P("row", "col"),
            P("row", "col", None, None),
            P("row", "col", None),
            P(),
            P(),
        ),
        out_specs=(P(None, "row", "col"), P()),
        check_vma=False,
    )
```

time: 78.2 us -> 60.7 us (0.78)
  Pallas kernels: 70.7 us -> 55.8 us
  local copies, waits for them, and re-layouts: 5.72 us -> 3.44 us
    pallas_call x3 -> x1, Pallas kernels: 70.7 us -> 55.8 us  [body(): pl.pallas_call(functools.partial(kernel, rows, cols, nx, n1, cap, mixes),...]
    unnamed x16 -> x2, local copies, waits for them, and re-layouts: 5.72 us -> 3.44 us
where the time goes in v2:
time: 60.7 us; the launch traced here: 60.5 us
  Pallas kernels  55.8 us (92%)
  local copies, waits for them, and re-layouts  3.44 us (6%)
  between operations  1.29 us (2%)
    pallas_call x1, Pallas kernels, body(): pl.pallas_call(functools.partial(kernel, rows, cols, nx, n1, cap, mixes),...  55.8 us
    unnamed x2, local copies, waits for them, and re-layouts  3.44 us

profile of v2, /device:TPU:1, one launch (start us, length us, event | category | flops | bytes accessed | tf_op | source)
XLA Modules:
  0.0 60.5 jit_solution(9786655490028972108)
XLA Ops:
  1.3 55.8 %update.1 = (f32[2,128,128]{2,1,0:T(8,128)}, f32[4,2,128,128]{3,2,1,0:T(8,128)}) custom-call(f32[2,128,128]{2,1,0:T(8,128)} %o_hbm.1, bf16[1,1,12,128,128]{4,3,2,1,0:T(8,128)(2,1)} %a_hbm.1, s32[1,1]{1,0:T(1,128)S(6)} %copy.12.counts_hbm, s32[1,1,2,12]{3,2,1,0:T(2,128)} %bitcast.3, s32[1,1,12]{2,1,0:T(1,128)} %index_hbm.1, f32[4,16]{1,0:T(4,128)} %bitcast.2, ...), custom_call_target="tpu_custom_call" | custom-call | tf_op jit(solution)/shard_map/update/pallas_call | solution.py:445
  57.1 1.6 %copy.13 = f32[2,128,128]{2,1,0:T(8,128)} copy(f32[2,128,128]{2,1,0:T(8,128)} %get-tuple-element.4) | data formatting | bytes 262144
  58.7 1.9 %copy.14 = f32[4,2,128,128]{3,2,1,0:T(8,128)} copy(f32[4,2,128,128]{3,2,1,0:T(8,128)} %get-tuple-element.5) | data formatting | bytes 1048576

commit v3 on v2

--- a/solution.py
+++ b/solution.py
@@ -84,10 +84,10 @@
 def kernel(
     rows, cols, nx, n1, cap, mixes,
     o_hbm, a_hbm, counts_hbm, offs_hbm, index_hbm, mix_hbm, modes_hbm, tab_hbm,
-    new_object, new_modes,
+    new_object, fresh,
     obj, amps, counts, offs, index, mix, modes, tab,
     ps, pc, rv, rs, rc, tiles, probes, patches, deltas, sums, pad, marg,
-    on, op, oc, orv, ors, orc, got, half, r1, r2, r3, fresh,
+    on, op, oc, orv, ors, orc, got, half, r1, r2, r3,
     load, send, recv,
 ):
     n = 128
@@ -187,16 +187,63 @@
         pick = jnp.clip(index[0, 0, slot], 0, mixes - 1)
         return [jnp.where(slot < count, mix[k, pick], 0.0) for k in range(4)]
 
-    def make_probe(slot, carry):
-        w = weights_of(slot)
-        for comp in range(2):
-            total = w[0] * modes[0, comp]
-            for k in range(1, 4):
-                total = total + w[k] * modes[k, comp]
-            probes[slot, comp] = total
+    def spread(frames, spots):
+        for f in frames:
+            for h in range(4):
+                part = slice(h * 64, (h + 1) * 64)
+                low, up = marg[f, 0, part], marg[f, 1, part]
+                for i, (top, left_px) in enumerate(spots):
+                    value = pad[i, f, pl.ds(n - top + h * 64, 64), :]
+                    mask = lanes_iota((64, n)) >= left_px
+                    low = low + jnp.where(mask, value, 0.0)
+                    up = up + jnp.where(mask, 0.0, value)
+                marg[f, 0, part] = low
+                marg[f, 1, part] = up
+
+    def centre(frames, part):
+        own, end = marg[frames, 0, part], marg[frames, 1, part]
+        return jnp.where(lanes_iota(own.shape) < 64, pltpu.roll(own, 64, 2), pltpu.roll(end, 64, 2))
+
+    def send_edges(frames):
+        top, middle, bottom = slice(0, 64), slice(64, 192), slice(192, 256)
+        on[0, frames] = centre(frames, top)
+        on[1, frames] = centre(frames, bottom)
+        op[0, frames] = pack_low(marg[frames, 0, middle])
+        op[1, frames] = pack_high(marg[frames, 1, middle])
+        oc[0, frames] = pack_low(marg[frames, 0, top])
+        oc[1, frames] = pack_high(marg[frames, 1, top])
+        oc[2, frames] = pack_low(marg[frames, 0, bottom])
+        oc[3, frames] = pack_high(marg[frames, 1, bottom])
+        return [
+            copy(oc.at[0, frames], orc.at[0, frames], around[-1, -1]),
+            copy(oc.at[1, frames], orc.at[1, frames], around[-1, 1]),
+            copy(oc.at[2, frames], orc.at[2, frames], around[1, -1]),
+            copy(oc.at[3, frames], orc.at[3, frames], around[1, 1]),
+            copy(on.at[0, frames], orv.at[0, frames], around[-1, 0]),
+            copy(on.at[1, frames], orv.at[1, frames], around[1, 0]),
+            copy(op.at[0, frames], ors.at[0, frames], around[0, -1]),
+            copy(op.at[1, frames], ors.at[1, frames], around[0, 1]),
+        ]
+
+    def make_probes(step, carry):
+        slots = [step * GROUP + i for i in range(GROUP)]
+        spots = [spot(slot) for slot in slots]
+        for i, slot in enumerate(slots):
+            w = weights_of(slot)
+            probe = []
+            for comp in range(2):
+                total = w[0] * modes[0, comp]
+                for k in range(1, 4):
+                    total = total + w[k] * modes[k, comp]
+                probes[slot, comp] = total
+                probe.append(total)
+            value = probe[0] * probe[0] + probe[1] * probe[1]
+            pad[i, 2, n : 2 * n] = pltpu.roll(value, spots[i][1], 1)
+        spread((2,), spots)
         return carry
 
-    lax.fori_loop(0, cap, make_probe, 0)
+    lax.fori_loop(0, cap // GROUP, make_probes, 0)
+    edge = send_edges(slice(2, 3))
     for c in halo:
         c.wait_recv()
 
@@ -299,41 +346,18 @@
         if d:
             sent.append(copy(half.at[:, :, chunk(a)], r1.at[d - 1], device))
 
-    def spread(step, carry):
+    def numerators(step, carry):
         slots = [step * GROUP + i for i in range(GROUP)]
         spots = [spot(slot) for slot in slots]
         for i, slot in enumerate(slots):
             pr, pi = probes[slot, 0], probes[slot, 1]
             dr, di = deltas[slot, 0], deltas[slot, 1]
-            for f, value in enumerate((pr * dr + pi * di, pr * di - pi * dr, pr * pr + pi * pi)):
+            for f, value in enumerate((pr * dr + pi * di, pr * di - pi * dr)):
                 pad[i, f, n : 2 * n] = pltpu.roll(value, spots[i][1], 1)
-        for f in range(3):
-            for h in range(4):
-                part = slice(h * 64, (h + 1) * 64)
-                low, up = marg[f, 0, part], marg[f, 1, part]
-                for i, (top, left_px) in enumerate(spots):
-                    value = pad[i, f, pl.ds(n - top + h * 64, 64), :]
-                    mask = lanes_iota((64, n)) >= left_px
-                    low = low + jnp.where(mask, value, 0.0)
-                    up = up + jnp.where(mask, 0.0, value)
-                marg[f, 0, part] = low
-                marg[f, 1, part] = up
+        spread((0, 1), spots)
         return carry
 
-    lax.fori_loop(0, cap // GROUP, spread, 0)
-    low64 = lanes_iota((3, 64, n)) < 64
-
-    def centre(part):
-        return jnp.where(low64, pltpu.roll(marg[:, 0, part], 64, 2), pltpu.roll(marg[:, 1, part], 64, 2))
-
-    on[0] = centre(slice(0, 64))
-    on[1] = centre(slice(192, 256))
-    op[0] = pack_low(marg[:, 0, 64:192])
-    op[1] = pack_high(marg[:, 1, 64:192])
-    oc[0] = pack_low(marg[:, 0, 0:64])
-    oc[1] = pack_high(marg[:, 1, 0:64])
-    oc[2] = pack_low(marg[:, 0, 192:256])
-    oc[3] = pack_high(marg[:, 1, 192:256])
+    lax.fori_loop(0, cap // GROUP, numerators, 0)
 
     mine = chunk(p1)
     total = half[:, :, mine]
@@ -348,16 +372,6 @@
     for d in range(1, nx):
         a, device = x_peer(d)
         sent.append(copy(r2.at[a], r2.at[nx + d - 1], device))
-    edge = [
-        copy(oc.at[0], orc.at[0], around[-1, -1]),
-        copy(oc.at[1], orc.at[1], around[-1, 1]),
-        copy(oc.at[2], orc.at[2], around[1, -1]),
-        copy(oc.at[3], orc.at[3], around[1, 1]),
-        copy(on.at[0], orv.at[0], around[-1, 0]),
-        copy(on.at[1], orv.at[1], around[1, 0]),
-        copy(op.at[0], ors.at[0], around[0, -1]),
-        copy(op.at[1], ors.at[1], around[0, 1]),
-    ]
     total = r2[x]
     for d, c in enumerate(sent):
         c.wait_recv()
@@ -367,6 +381,7 @@
     for d in FAR:
         _, device = second_peer(d)
         sent.append(copy(r3.at[p2], r3.at[p2], device))
+    edge += send_edges(slice(0, 2))
     for c in sent:
         c.wait_recv()
     total = r3[0]
@@ -396,8 +411,8 @@
         (slice(0, 64), slice(64, 128), orv[1] * ok(-1, 0), orc[3] * ok(-1, -1), orc[2] * ok(-1, 1)),
         (slice(64, 128), slice(128, 192), orv[0] * ok(1, 0), orc[1] * ok(1, -1), orc[0] * ok(1, 1)),
     ):
-        side = jnp.where(low64, west[:, part] + unpack_low(lo), east[:, part] + unpack_high(up))
-        both_sums = centre(inner) + vertical + side
+        side = jnp.where(lanes_iota((3, 64, n)) < 64, west[:, part] + unpack_low(lo), east[:, part] + unpack_high(up))
+        both_sums = centre(slice(0, 3), inner) + vertical + side
         new_object[:, part] = obj[:, part] + both_sums[:2] / (both_sums[2:] + RELAX)
 
     for d in NEAR:
@@ -407,7 +422,15 @@
     for c in pair:
         c.wait_recv()
 
-    scale = 1.0 / (n * n)
+    for c in pending:
+        c.wait_send()
+
+
+def finish_kernel(object_in, fresh, object_out, modes_out, made, sem):
+    first = pltpu.make_async_copy(object_in, object_out, sem.at[0])
+    first.start()
+    copies = [first]
+    scale = 1.0 / (fresh.shape[2] * fresh.shape[3])
 
     def mean(v):
         return jnp.sum(jnp.sum(v, 0, keepdims=True), 1, keepdims=True) * scale
@@ -424,13 +447,16 @@
         norm = 1.0 / jnp.sqrt(mean(vr * vr + vi * vi) + EPSILON)
         qr, qi = vr * norm, vi * norm
         basis.append((qr, qi))
-        new_modes[k, 0] = qr
-        new_modes[k, 1] = qi
+        made[k, 0] = qr
+        made[k, 1] = qi
+        write = pltpu.make_async_copy(made.at[k], modes_out.at[k], sem.at[k + 1])
+        write.start()
+        copies.append(write)
         for later in range(k + 1, 4):
             fr, fi = fresh[later, 0], fresh[later, 1]
             coefs[k, later] = (mean(qr * fr + qi * fi), mean(qr * fi - qi * fr))
-    for c in pending:
-        c.wait_send()
+    for c in copies:
+        c.wait()
 
 
 def solution(mesh):
@@ -441,12 +467,12 @@
 
     def body(object_field, amplitudes, counts, offsets, mode_index, mix_table, probe_modes):
         cap, mixes = amplitudes.shape[2], mix_table.shape[0]
-        number = 16 + 8 + 8 + 3 * (n1 - 1) + 2 * (nx - 1)
-        return pl.pallas_call(
+        number = 16 + 16 + 8 + 3 * (n1 - 1) + 2 * (nx - 1)
+        new_object, fresh = pl.pallas_call(
             functools.partial(kernel, rows, cols, nx, n1, cap, mixes),
             out_shape=(
-                jax.ShapeDtypeStruct((2, 128, 128), f32),
-                jax.ShapeDtypeStruct((4, 2, 128, 128), f32),
+                pltpu.VMEM((2, 128, 128), f32),
+                pltpu.VMEM((4, 2, 128, 128), f32),
             ),
             in_specs=[HBM] * 8,
             out_specs=(VMEM, VMEM),
@@ -482,7 +508,6 @@
                 pltpu.VMEM((n1 - 1, 2, 3, 128 // n1, 128), f32),
                 pltpu.VMEM((2 * nx, 3, 8, 128), f32),
                 pltpu.VMEM((n1, 3, 8, 128), f32),
-                pltpu.VMEM((4, 2, 128, 128), f32),
                 pltpu.SemaphoreType.DMA((8,)),
                 pltpu.SemaphoreType.DMA((number,)),
                 pltpu.SemaphoreType.DMA((number,)),
@@ -495,6 +520,18 @@
             object_field, amplitudes, counts, jnp.swapaxes(offsets, 2, 3), mode_index, mix_table.T,
             probe_modes, jnp.asarray(tables(128)),
         )
+        return pl.pallas_call(
+            finish_kernel,
+            out_shape=(
+                jax.ShapeDtypeStruct((2, 128, 128), f32),
+                jax.ShapeDtypeStruct((4, 2, 128, 128), f32),
+            ),
+            in_specs=[VMEM, VMEM],
+            out_specs=(HBM, HBM),
+            scratch_shapes=[pltpu.VMEM((4, 2, 128, 128), f32), pltpu.SemaphoreType.DMA((5,))],
+            compiler_params=pltpu.CompilerParams(vmem_limit_bytes=8 * 1024 * 1024),
+            name="finish",
+        )(new_object, fresh)
 
     return jax.shard_map(
         body,

time: 60.7 us -> 58.2 us (0.959)
  local copies, waits for them, and re-layouts: 3.44 us -> 0 us
  Pallas kernels: 55.8 us -> 56.8 us
    unnamed x2 -> x0, local copies, waits for them, and re-layouts: 3.44 us -> none
    pallas_call x0 -> x1, Pallas kernels: none -> 1.58 us  [body(): pl.pallas_call(finish_kernel, out_shape=(jax.ShapeDtypeStruct((2, 128, 12...]
    pallas_call x1, Pallas kernels: 55.8 us -> 55.2 us  [body(): pl.pallas_call(functools.partial(kernel, rows, cols, nx, n1, cap, mixes),...]
where the time goes in v3:
time: 58.2 us; the launch traced here: 58 us
  Pallas kernels  56.8 us (98%)
  between operations  1.28 us (2%)
    pallas_call x1, Pallas kernels, body(): pl.pallas_call(functools.partial(kernel, rows, cols, nx, n1, cap, mixes),...  55.2 us
    pallas_call x1, Pallas kernels, body(): pl.pallas_call(finish_kernel, out_shape=(jax.ShapeDtypeStruct((2, 128, 12...  1.58 us

profile of v3, /device:TPU:1, one launch (start us, length us, event | category | flops | bytes accessed | tf_op | source)
XLA Modules:
  0.0 58.0 jit_solution(10285182308274451206)
XLA Ops:
  1.3 55.2 %update.1 = (f32[2,128,128]{2,1,0:T(8,128)S(1)}, f32[4,2,128,128]{3,2,1,0:T(8,128)S(1)}) custom-call(f32[2,128,128]{2,1,0:T(8,128)} %o_hbm.1, bf16[1,1,12,128,128]{4,3,2,1,0:T(8,128)(2,1)} %a_hbm.1, s32[1,1]{1,0:T(1,128)S(6)} %copy.10.counts_hbm, s32[1,1,2,12]{3,2,1,0:T(2,128)} %bitcast.3, s32[1,1,12]{2,1,0:T(1,128)} %index_hbm.1, f32[4,16]{1,0:T(4,128)} %bitcast.2, ...), custom_call_target="tpu_custom_call" | custom-call | tf_op jit(solution)/shard_map/update/pallas_call | solution.py:471
  56.5 1.6 %finish.1 = (f32[2,128,128]{2,1,0:T(8,128)}, f32[4,2,128,128]{3,2,1,0:T(8,128)}) custom-call(f32[2,128,128]{2,1,0:T(8,128)S(1)} %get-tuple-element.4.object_in, f32[4,2,128,128]{3,2,1,0:T(8,128)S(1)} %get-tuple-element.5.fresh), custom_call_target="tpu_custom_call" | custom-call | tf_op jit(solution)/shard_map/finish/pallas_call | solution.py:523

commit v4 on v3

--- a/solution.py
+++ b/solution.py
@@ -13,6 +13,7 @@
 RELAX = 0.5
 EPSILON = 1e-06
 GROUP = 2
+TEAM = 6
 FAR = (4, 3, 5, 2, 6, 1, 7)
 NEAR = (1, 7, 2, 6, 3, 5, 4)
 MESH = pl.DeviceIdType.MESH
@@ -86,9 +87,9 @@
     o_hbm, a_hbm, counts_hbm, offs_hbm, index_hbm, mix_hbm, modes_hbm, tab_hbm,
     new_object, fresh,
     obj, amps, counts, offs, index, mix, modes, tab,
-    ps, pc, rv, rs, rc, tiles, probes, patches, deltas, sums, pad, marg,
+    ps, pc, rv, rs, rc, tiles, probes, patches, psis, backs, deltas, sums, pad, marg,
     on, op, oc, orv, ors, orc, got, half, r1, r2, r3,
-    load, send, recv,
+    load, send, recv, pair_send, pair_recv,
 ):
     n = 128
     nz = rows // nx
@@ -174,7 +175,6 @@
     for c in loads[1:]:
         c.wait()
     marg[...] = jnp.zeros_like(marg)
-    sums[...] = jnp.zeros_like(sums)
     pad[...] = jnp.zeros_like(pad)
     count = counts[0, 0]
 
@@ -286,7 +286,7 @@
     lane = lanes_iota((n, n))
 
     def visit(step, carry):
-        slots = [step * GROUP + i for i in range(GROUP)]
+        slots = [step * TEAM + i for i in range(TEAM)]
         psi_r, psi_i = [], []
         for slot in slots:
             top, left_px = spot(slot)
@@ -298,9 +298,13 @@
                 patch.append(pltpu.roll(jnp.where(mask, a, b), lax.rem(n - left_px, n), 1))
                 patches[slot, comp] = patch[comp]
             pr, pi = probes[slot, 0], probes[slot, 1]
-            psi_r.append(pr * patch[0] - pi * patch[1])
-            psi_i.append(pr * patch[1] + pi * patch[0])
-        re, im = left(fwd, lower(psi_r), lower(psi_i))
+            real = pr * patch[0] - pi * patch[1]
+            imag = pr * patch[1] + pi * patch[0]
+            psis[slot, 0] = real
+            psis[slot, 1] = imag
+            psi_r.append(real.astype(jnp.bfloat16))
+            psi_i.append(imag.astype(jnp.bfloat16))
+        re, im = left(fwd, psi_r, psi_i)
         re, im = right(inv, lower(re), lower(im))
         fixed_re, fixed_im = [], []
         for slot, a, b in zip(slots, re, im):
@@ -308,38 +312,54 @@
             fixed_re.append((a * ratio).astype(jnp.bfloat16))
             fixed_im.append((b * ratio).astype(jnp.bfloat16))
         re, im = left(inv, fixed_re, fixed_im)
-        re, im = right(fwd, lower(re), lower(im))
-        pieces, weights = [], []
-        for i, slot in enumerate(slots):
-            dr, di = re[i] - psi_r[i], im[i] - psi_i[i]
-            deltas[slot, 0] = dr
-            deltas[slot, 1] = di
-            ar, ai = patches[slot, 0], patches[slot, 1]
-            pieces.append((ar * dr + ai * di, ar * di - ai * dr, ar * ar + ai * ai))
-            weights.append(weights_of(slot))
+        for slot, a, b in zip(slots, lower(re), lower(im)):
+            backs[slot, :, :n] = a
+            backs[slot, :, n:] = b
+        return carry
+
+    lax.fori_loop(0, cap // TEAM, visit, 0)
+
+    thick = n // n1
+
+    def chunk(a):
+        return pl.ds(pl.multiple_of(a * thick, thick), thick)
+
+    def pair_copy(i, d):
+        piece = chunk(lax.rem(p2 + d, n1))
+        return pltpu.make_async_remote_copy(
+            src_ref=sums.at[pl.ds(other, 2), :, piece], dst_ref=got.at[:, :, piece],
+            send_sem=pair_send.at[i], recv_sem=pair_recv.at[i], device_id=sibling, device_id_type=MESH,
+        )
+
+    def finish_rows(i, carry):
+        d = n1 // 2 + (1 - 2 * lax.rem(i, 2)) * ((i + 1) // 2)
+        rows_here = chunk(lax.rem(p2 + d, n1))
+        out = dot(backs[:, rows_here, :].reshape(cap * thick, 2 * n), fwd)
+        totals = [[jnp.zeros((thick, n), jnp.float32) for _ in range(3)] for _ in range(4)]
+        for slot in range(cap):
+            part = slice(slot * thick, (slot + 1) * thick)
+            dr = out[part, :n] - psis[slot, 0, rows_here]
+            di = out[part, n:] - psis[slot, 1, rows_here]
+            deltas[slot, 0, rows_here] = dr
+            deltas[slot, 1, rows_here] = di
+            ar, ai = patches[slot, 0, rows_here], patches[slot, 1, rows_here]
+            pieces = (ar * dr + ai * di, ar * di - ai * dr, ar * ar + ai * ai)
+            w = weights_of(slot)
+            for k in range(4):
+                totals[k][0] = totals[k][0] + w[k] * pieces[0]
+                totals[k][1] = totals[k][1] + w[k] * pieces[1]
+                totals[k][2] = totals[k][2] + (w[k] * w[k]) * pieces[2]
         for k in range(4):
             for f in range(3):
-                total = sums[k, f]
-                for i in range(GROUP):
-                    w = weights[i][k]
-                    total = total + (w if f < 2 else w * w) * pieces[i][f]
-                sums[k, f] = total
+                sums[k, f, rows_here] = totals[k][f]
+        pair_copy(i, d).start()
         return carry
 
-    lax.fori_loop(0, cap // GROUP, visit, 0)
-
-    thick = n // n1
-
-    def chunk(a):
-        return pl.ds(pl.multiple_of(a * thick, thick), thick)
-
+    lax.fori_loop(0, n1, finish_rows, 0)
     order = FAR + (0,)
-    pair = []
-    for d in order:
-        piece = chunk(lax.rem(p2 + d, n1))
-        pair.append(copy(sums.at[pl.ds(other, 2), :, piece], got.at[:, :, piece], sibling))
+    pair_out = [pair_copy(i, d) for i, d in enumerate(order)]
     sent = []
-    for d, c in zip(order, pair):
+    for d, c in zip(order, pair_out):
         c.wait_recv()
         a, device = first_peer(d)
         half[:, :, chunk(a)] = sums[pl.ds(high, 2), :, chunk(a)] + got[:, :, chunk(a)]
@@ -422,7 +442,7 @@
     for c in pair:
         c.wait_recv()
 
-    for c in pending:
+    for c in pending + pair_out:
         c.wait_send()
 
 
@@ -467,7 +487,7 @@
 
     def body(object_field, amplitudes, counts, offsets, mode_index, mix_table, probe_modes):
         cap, mixes = amplitudes.shape[2], mix_table.shape[0]
-        number = 16 + 16 + 8 + 3 * (n1 - 1) + 2 * (nx - 1)
+        number = 8 + 16 + 8 + 3 * (n1 - 1) + 2 * (nx - 1)
         new_object, fresh = pl.pallas_call(
             functools.partial(kernel, rows, cols, nx, n1, cap, mixes),
             out_shape=(
@@ -494,6 +514,8 @@
                 pltpu.VMEM((cap, 2, 128, 128), f32),
                 pltpu.VMEM((cap, 2, 128, 128), f32),
                 pltpu.VMEM((cap, 2, 128, 128), f32),
+                pltpu.VMEM((cap, 128, 256), bf16),
+                pltpu.VMEM((cap, 2, 128, 128), f32),
                 pltpu.VMEM((4, 3, 128, 128), f32),
                 pltpu.VMEM((GROUP, 3, 384, 128), f32),
                 pltpu.VMEM((3, 2, 256, 128), f32),
@@ -511,6 +533,8 @@
                 pltpu.SemaphoreType.DMA((8,)),
                 pltpu.SemaphoreType.DMA((number,)),
                 pltpu.SemaphoreType.DMA((number,)),
+                pltpu.SemaphoreType.DMA((n1,)),
+                pltpu.SemaphoreType.DMA((n1,)),
             ],
             compiler_params=pltpu.CompilerParams(
                 collective_id=0, has_side_effects=True, vmem_limit_bytes=56 * 1024 * 1024

time: 58.2 us -> 56.3 us (0.967)
  Pallas kernels: 56.8 us -> 54.9 us
    pallas_call x1, Pallas kernels: 55.2 us -> 53.3 us  [body(): pl.pallas_call(functools.partial(kernel, rows, cols, nx, n1, cap, mixes),...]
where the time goes in v4:
time: 56.3 us; the launch traced here: 56.2 us
  Pallas kernels  54.9 us (98%)
  between operations  1.28 us (2%)
    pallas_call x1, Pallas kernels, body(): pl.pallas_call(functools.partial(kernel, rows, cols, nx, n1, cap, mixes),...  53.3 us
    pallas_call x1, Pallas kernels, body(): pl.pallas_call(finish_kernel, out_shape=(jax.ShapeDtypeStruct((2, 128, 12...  1.58 us

profile of v4, /device:TPU:1, one launch (start us, length us, event | category | flops | bytes accessed | tf_op | source)
XLA Modules:
  0.0 56.2 jit_solution(2985582305789153309)
XLA Ops:
  1.3 53.3 %update.1 = (f32[2,128,128]{2,1,0:T(8,128)S(1)}, f32[4,2,128,128]{3,2,1,0:T(8,128)S(1)}) custom-call(f32[2,128,128]{2,1,0:T(8,128)} %o_hbm.1, bf16[1,1,12,128,128]{4,3,2,1,0:T(8,128)(2,1)} %a_hbm.1, s32[1,1]{1,0:T(1,128)S(6)} %copy.10.counts_hbm, s32[1,1,2,12]{3,2,1,0:T(2,128)} %bitcast.3, s32[1,1,12]{2,1,0:T(1,128)} %index_hbm.1, f32[4,16]{1,0:T(4,128)} %bitcast.2, ...), custom_call_target="tpu_custom_call" | custom-call | tf_op jit(solution)/shard_map/update/pallas_call | solution.py:491
  54.6 1.6 %finish.1 = (f32[2,128,128]{2,1,0:T(8,128)}, f32[4,2,128,128]{3,2,1,0:T(8,128)}) custom-call(f32[2,128,128]{2,1,0:T(8,128)S(1)} %get-tuple-element.4.object_in, f32[4,2,128,128]{3,2,1,0:T(8,128)S(1)} %get-tuple-element.5.fresh), custom_call_target="tpu_custom_call" | custom-call | tf_op jit(solution)/shard_map/finish/pallas_call | solution.py:547

commit v5 on v4

--- a/solution.py
+++ b/solution.py
@@ -13,7 +13,7 @@
 RELAX = 0.5
 EPSILON = 1e-06
 GROUP = 2
-TEAM = 6
+TEAM = 12
 FAR = (4, 3, 5, 2, 6, 1, 7)
 NEAR = (1, 7, 2, 6, 3, 5, 4)
 MESH = pl.DeviceIdType.MESH
@@ -358,13 +358,21 @@
     lax.fori_loop(0, n1, finish_rows, 0)
     order = FAR + (0,)
     pair_out = [pair_copy(i, d) for i, d in enumerate(order)]
-    sent = []
+    streams = (0, 1)
+    sent = [[], []]
+
+    def send_first(m, d):
+        a, device = first_peer(d)
+        sent[m].append(copy(half.at[m, :, chunk(a)], r1.at[m, d - 1], device))
+
     for d, c in zip(order, pair_out):
         c.wait_recv()
-        a, device = first_peer(d)
+        a, _ = first_peer(d)
         half[:, :, chunk(a)] = sums[pl.ds(high, 2), :, chunk(a)] + got[:, :, chunk(a)]
         if d:
-            sent.append(copy(half.at[:, :, chunk(a)], r1.at[d - 1], device))
+            send_first(0, d)
+    for d in FAR:
+        send_first(1, d)
 
     def numerators(step, carry):
         slots = [step * GROUP + i for i in range(GROUP)]
@@ -380,48 +388,54 @@
     lax.fori_loop(0, cap // GROUP, numerators, 0)
 
     mine = chunk(p1)
-    total = half[:, :, mine]
-    for d, c in zip(FAR[::-1], sent[::-1]):
-        c.wait_recv()
-        total = total + r1[d - 1]
-    parts = thick // 8
-    for m in range(2):
-        for t in range(parts):
-            r2[m * parts + t] = total[m, :, t * 8 : (t + 1) * 8]
-    sent = []
-    for d in range(1, nx):
-        a, device = x_peer(d)
-        sent.append(copy(r2.at[a], r2.at[nx + d - 1], device))
-    total = r2[x]
-    for d, c in enumerate(sent):
-        c.wait_recv()
-        total = total + r2[nx + d]
-    r3[p2] = total
-    sent = []
-    for d in FAR:
-        _, device = second_peer(d)
-        sent.append(copy(r3.at[p2], r3.at[p2], device))
+    parity = lax.rem(x, 2)
+    x_sent = [[], []]
+    for m in streams:
+        total = half[m, :, mine]
+        for d, c in zip(FAR[::-1], sent[m][::-1]):
+            c.wait_recv()
+            total = total + r1[m, d - 1]
+        for t in range(2):
+            r2[m, t] = total[:, t * 8 : (t + 1) * 8]
+        r2[m, 2 + x] = r2[m, parity]
+        for d in range(1, nx):
+            a, device = x_peer(d)
+            x_sent[m].append(copy(r2.at[m, lax.rem(a, 2)], r2.at[m, 2 + x], device))
+    second_sent = [[], []]
+    for m in streams:
+        for c in x_sent[m]:
+            c.wait_recv()
+        total = r2[m, 2]
+        for a in range(1, nx):
+            total = total + r2[m, 2 + a]
+        r3[m, p2] = total
+        for d in FAR:
+            _, device = second_peer(d)
+            second_sent[m].append(copy(r3.at[m, p2], r3.at[m, p2], device))
     edge += send_edges(slice(0, 2))
-    for c in sent:
-        c.wait_recv()
-    total = r3[0]
-    for a in range(1, n1):
-        total = total + r3[a]
-    mode, tile = high + x // parts, lax.rem(x, parts)
-    unit = pl.ds(pl.multiple_of(p1 * thick + tile * 8, 8), 8)
-    fresh[mode, :, unit] = modes[mode, :, unit] + total[:2] / (total[2:] + RELAX)
-    sent = []
-    for d in range(1, nx):
-        _, device = x_peer(d)
-        sent.append(copy(fresh.at[mode, :, unit], fresh.at[mode, :, unit], device))
-    for c in sent:
-        c.wait_recv()
-    both = pl.ds(high, 2)
-    sent = {}
-    for d in FAR:
-        _, device = first_peer(d)
-        sent[d] = copy(fresh.at[both, :, mine], fresh.at[both, :, mine], device)
-    pair = [copy(fresh.at[both, :, mine], fresh.at[both, :, mine], sibling)]
+    unit = pl.ds(pl.multiple_of(p1 * thick + parity * 8, 8), 8)
+    back_sent = []
+    partner = ((x + 1 - 2 * parity) * nz + z, col)
+    for m in streams:
+        for c in second_sent[m]:
+            c.wait_recv()
+        total = r3[m, 0]
+        for a in range(1, n1):
+            total = total + r3[m, a]
+        fresh[high + m, :, unit] = modes[high + m, :, unit] + total[:2] / (total[2:] + RELAX)
+        here = fresh.at[high + m, :, unit]
+        back_sent.append(copy(here, here, partner))
+    gather = []
+    for m in streams:
+        back_sent[m].wait_recv()
+        here = fresh.at[high + m, :, mine]
+        to_peers = {}
+        for d in FAR:
+            _, device = first_peer(d)
+            to_peers[d] = copy(here, here, device)
+        gather.append(to_peers)
+    here = fresh.at[high + 1, :, mine]
+    pair = [copy(here, here, sibling)]
 
     for c in edge:
         c.wait_recv()
@@ -436,9 +450,12 @@
         new_object[:, part] = obj[:, part] + both_sums[:2] / (both_sums[2:] + RELAX)
 
     for d in NEAR:
-        sent[d].wait_recv()
-        piece = chunk(lax.rem(p1 + n1 - d, n1))
-        pair.append(copy(fresh.at[both, :, piece], fresh.at[both, :, piece], sibling))
+        gather[0][d].wait_recv()
+    pair.append(copy(fresh.at[high], fresh.at[high], sibling))
+    for d in NEAR:
+        gather[1][d].wait_recv()
+        here = fresh.at[high + 1, :, chunk(lax.rem(p1 + n1 - d, n1))]
+        pair.append(copy(here, here, sibling))
     for c in pair:
         c.wait_recv()
 
@@ -487,7 +504,7 @@
 
     def body(object_field, amplitudes, counts, offsets, mode_index, mix_table, probe_modes):
         cap, mixes = amplitudes.shape[2], mix_table.shape[0]
-        number = 8 + 16 + 8 + 3 * (n1 - 1) + 2 * (nx - 1)
+        number = 24 + 6 * (n1 - 1) + 2 * (nx - 1) + 2 + n1 + 1
         new_object, fresh = pl.pallas_call(
             functools.partial(kernel, rows, cols, nx, n1, cap, mixes),
             out_shape=(
@@ -527,9 +544,9 @@
                 pltpu.VMEM((4, 3, 32, 128), f32),
                 pltpu.VMEM((2, 3, 128, 128), f32),
                 pltpu.VMEM((2, 3, 128, 128), f32),
-                pltpu.VMEM((n1 - 1, 2, 3, 128 // n1, 128), f32),
-                pltpu.VMEM((2 * nx, 3, 8, 128), f32),
-                pltpu.VMEM((n1, 3, 8, 128), f32),
+                pltpu.VMEM((2, n1 - 1, 3, 128 // n1, 128), f32),
+                pltpu.VMEM((2, 2 + nx, 3, 8, 128), f32),
+                pltpu.VMEM((2, n1, 3, 8, 128), f32),
                 pltpu.SemaphoreType.DMA((8,)),
                 pltpu.SemaphoreType.DMA((number,)),
                 pltpu.SemaphoreType.DMA((number,)),

time: 56.3 us -> 54.4 us (0.966)
  Pallas kernels: 54.9 us -> 53 us
    pallas_call x1, Pallas kernels: 53.3 us -> 51.4 us  [body(): pl.pallas_call(functools.partial(kernel, rows, cols, nx, n1, cap, mixes),...]
where the time goes in v5:
time: 54.4 us; the launch traced here: 54.2 us
  Pallas kernels  53 us (97%)
  between operations  1.28 us (2%)
    pallas_call x1, Pallas kernels, body(): pl.pallas_call(functools.partial(kernel, rows, cols, nx, n1, cap, mixes),...  51.4 us
    pallas_call x1, Pallas kernels, body(): pl.pallas_call(finish_kernel, out_shape=(jax.ShapeDtypeStruct((2, 128, 12...  1.58 us

profile of v5, /device:TPU:1, one launch (start us, length us, event | category | flops | bytes accessed | tf_op | source)
XLA Modules:
  0.0 54.2 jit_solution(16588947328951206268)
XLA Ops:
  1.3 51.4 %update.1 = (f32[2,128,128]{2,1,0:T(8,128)S(1)}, f32[4,2,128,128]{3,2,1,0:T(8,128)S(1)}) custom-call(f32[2,128,128]{2,1,0:T(8,128)} %o_hbm.1, bf16[1,1,12,128,128]{4,3,2,1,0:T(8,128)(2,1)} %a_hbm.1, s32[1,1]{1,0:T(1,128)S(6)} %copy.10.counts_hbm, s32[1,1,2,12]{3,2,1,0:T(2,128)} %bitcast.3, s32[1,1,12]{2,1,0:T(1,128)} %index_hbm.1, f32[4,16]{1,0:T(4,128)} %bitcast.2, ...), custom_call_target="tpu_custom_call" | custom-call | tf_op jit(solution)/shard_map/update/pallas_call | solution.py:508
  52.7 1.6 %finish.1 = (f32[2,128,128]{2,1,0:T(8,128)}, f32[4,2,128,128]{3,2,1,0:T(8,128)}) custom-call(f32[2,128,128]{2,1,0:T(8,128)S(1)} %get-tuple-element.4.object_in, f32[4,2,128,128]{3,2,1,0:T(8,128)S(1)} %get-tuple-element.5.fresh), custom_call_target="tpu_custom_call" | custom-call | tf_op jit(solution)/shard_map/finish/pallas_call | solution.py:564

commit v6 on v5

--- a/solution.py
+++ b/solution.py
@@ -87,7 +87,7 @@
     o_hbm, a_hbm, counts_hbm, offs_hbm, index_hbm, mix_hbm, modes_hbm, tab_hbm,
     new_object, fresh,
     obj, amps, counts, offs, index, mix, modes, tab,
-    ps, pc, rv, rs, rc, tiles, probes, patches, psis, backs, deltas, sums, pad, marg,
+    ps, pc, rv, rs, rc, tiles, probes, patches, deltas, splats, sums, pad, marg,
     on, op, oc, orv, ors, orc, got, half, r1, r2, r3,
     load, send, recv, pair_send, pair_recv,
 ):
@@ -230,6 +230,9 @@
         spots = [spot(slot) for slot in slots]
         for i, slot in enumerate(slots):
             w = weights_of(slot)
+            for k in range(4):
+                splats[slot, k : k + 1] = jnp.broadcast_to(w[k], (1, n))
+                splats[slot, 4 + k : 5 + k] = jnp.broadcast_to(w[k] * w[k], (1, n))
             probe = []
             for comp in range(2):
                 total = w[0] * modes[0, comp]
@@ -300,11 +303,9 @@
             pr, pi = probes[slot, 0], probes[slot, 1]
             real = pr * patch[0] - pi * patch[1]
             imag = pr * patch[1] + pi * patch[0]
-            psis[slot, 0] = real
-            psis[slot, 1] = imag
-            psi_r.append(real.astype(jnp.bfloat16))
-            psi_i.append(imag.astype(jnp.bfloat16))
-        re, im = left(fwd, psi_r, psi_i)
+            psi_r.append(real)
+            psi_i.append(imag)
+        re, im = left(fwd, lower(psi_r), lower(psi_i))
         re, im = right(inv, lower(re), lower(im))
         fixed_re, fixed_im = [], []
         for slot, a, b in zip(slots, re, im):
@@ -312,9 +313,10 @@
             fixed_re.append((a * ratio).astype(jnp.bfloat16))
             fixed_im.append((b * ratio).astype(jnp.bfloat16))
         re, im = left(inv, fixed_re, fixed_im)
-        for slot, a, b in zip(slots, lower(re), lower(im)):
-            backs[slot, :, :n] = a
-            backs[slot, :, n:] = b
+        re, im = right(fwd, lower(re), lower(im))
+        for i, slot in enumerate(slots):
+            deltas[slot, 0] = re[i] - psi_r[i]
+            deltas[slot, 1] = im[i] - psi_i[i]
         return carry
 
     lax.fori_loop(0, cap // TEAM, visit, 0)
@@ -334,21 +336,16 @@
     def finish_rows(i, carry):
         d = n1 // 2 + (1 - 2 * lax.rem(i, 2)) * ((i + 1) // 2)
         rows_here = chunk(lax.rem(p2 + d, n1))
-        out = dot(backs[:, rows_here, :].reshape(cap * thick, 2 * n), fwd)
         totals = [[jnp.zeros((thick, n), jnp.float32) for _ in range(3)] for _ in range(4)]
         for slot in range(cap):
-            part = slice(slot * thick, (slot + 1) * thick)
-            dr = out[part, :n] - psis[slot, 0, rows_here]
-            di = out[part, n:] - psis[slot, 1, rows_here]
-            deltas[slot, 0, rows_here] = dr
-            deltas[slot, 1, rows_here] = di
+            dr, di = deltas[slot, 0, rows_here], deltas[slot, 1, rows_here]
             ar, ai = patches[slot, 0, rows_here], patches[slot, 1, rows_here]
             pieces = (ar * dr + ai * di, ar * di - ai * dr, ar * ar + ai * ai)
-            w = weights_of(slot)
             for k in range(4):
-                totals[k][0] = totals[k][0] + w[k] * pieces[0]
-                totals[k][1] = totals[k][1] + w[k] * pieces[1]
-                totals[k][2] = totals[k][2] + (w[k] * w[k]) * pieces[2]
+                w, square = splats[slot, k : k + 1], splats[slot, 4 + k : 5 + k]
+                totals[k][0] = totals[k][0] + w * pieces[0]
+                totals[k][1] = totals[k][1] + w * pieces[1]
+                totals[k][2] = totals[k][2] + square * pieces[2]
         for k in range(4):
             for f in range(3):
                 sums[k, f, rows_here] = totals[k][f]
@@ -531,8 +528,7 @@
                 pltpu.VMEM((cap, 2, 128, 128), f32),
                 pltpu.VMEM((cap, 2, 128, 128), f32),
                 pltpu.VMEM((cap, 2, 128, 128), f32),
-                pltpu.VMEM((cap, 128, 256), bf16),
-                pltpu.VMEM((cap, 2, 128, 128), f32),
+                pltpu.VMEM((cap, 8, 128), f32),
                 pltpu.VMEM((4, 3, 128, 128), f32),
                 pltpu.VMEM((GROUP, 3, 384, 128), f32),
                 pltpu.VMEM((3, 2, 256, 128), f32),

time: 54.4 us -> 53.8 us (0.989)
  Pallas kernels: 53 us -> 52.4 us
    pallas_call x1, Pallas kernels: 51.4 us -> 50.8 us  [body(): pl.pallas_call(functools.partial(kernel, rows, cols, nx, n1, cap, mixes),...]
where the time goes in v6:
time: 53.8 us; the launch traced here: 53.7 us
  Pallas kernels  52.4 us (97%)
  between operations  1.28 us (2%)
    pallas_call x1, Pallas kernels, body(): pl.pallas_call(functools.partial(kernel, rows, cols, nx, n1, cap, mixes),...  50.8 us
    pallas_call x1, Pallas kernels, body(): pl.pallas_call(finish_kernel, out_shape=(jax.ShapeDtypeStruct((2, 128, 12...  1.58 us

profile of v6, /device:TPU:1, one launch (start us, length us, event | category | flops | bytes accessed | tf_op | source)
XLA Modules:
  0.0 53.7 jit_solution(16970537095255994335)
XLA Ops:
  1.3 50.8 %update.1 = (f32[2,128,128]{2,1,0:T(8,128)S(1)}, f32[4,2,128,128]{3,2,1,0:T(8,128)S(1)}) custom-call(f32[2,128,128]{2,1,0:T(8,128)} %o_hbm.1, bf16[1,1,12,128,128]{4,3,2,1,0:T(8,128)(2,1)} %a_hbm.1, s32[1,1]{1,0:T(1,128)S(6)} %copy.10.counts_hbm, s32[1,1,2,12]{3,2,1,0:T(2,128)} %bitcast.3, s32[1,1,12]{2,1,0:T(1,128)} %index_hbm.1, f32[4,16]{1,0:T(4,128)} %bitcast.2, ...), custom_call_target="tpu_custom_call" | custom-call | tf_op jit(solution)/shard_map/update/pallas_call | solution.py:505
  52.1 1.6 %finish.1 = (f32[2,128,128]{2,1,0:T(8,128)}, f32[4,2,128,128]{3,2,1,0:T(8,128)}) custom-call(f32[2,128,128]{2,1,0:T(8,128)S(1)} %get-tuple-element.4.object_in, f32[4,2,128,128]{3,2,1,0:T(8,128)S(1)} %get-tuple-element.5.fresh), custom_call_target="tpu_custom_call" | custom-call | tf_op jit(solution)/shard_map/finish/pallas_call | solution.py:560

commit v7 on v6

--- a/solution.py
+++ b/solution.py
@@ -127,6 +127,12 @@
         made.start()
         pending.append(made)
         return made
+
+    def flush(copies):
+        for c in copies:
+            c.wait_send()
+        done = [id(c) for c in copies]
+        pending[:] = [c for c in pending if id(c) not in done]
 
     def ok(dr, dc):
         return inside(row, col, rows, cols, dr, dc)
@@ -383,54 +389,47 @@
         return carry
 
     lax.fori_loop(0, cap // GROUP, numerators, 0)
+    flush(pair_out + halo + edge)
 
     mine = chunk(p1)
-    parity = lax.rem(x, 2)
     x_sent = [[], []]
     for m in streams:
         total = half[m, :, mine]
         for d, c in zip(FAR[::-1], sent[m][::-1]):
             c.wait_recv()
             total = total + r1[m, d - 1]
-        for t in range(2):
-            r2[m, t] = total[:, t * 8 : (t + 1) * 8]
-        r2[m, 2 + x] = r2[m, parity]
+        r2[m, x] = total
         for d in range(1, nx):
-            a, device = x_peer(d)
-            x_sent[m].append(copy(r2.at[m, lax.rem(a, 2)], r2.at[m, 2 + x], device))
+            _, device = x_peer(d)
+            x_sent[m].append(copy(r2.at[m, x], r2.at[m, x], device))
     second_sent = [[], []]
     for m in streams:
         for c in x_sent[m]:
             c.wait_recv()
-        total = r2[m, 2]
+        total = r2[m, 0]
         for a in range(1, nx):
-            total = total + r2[m, 2 + a]
+            total = total + r2[m, a]
         r3[m, p2] = total
         for d in FAR:
             _, device = second_peer(d)
             second_sent[m].append(copy(r3.at[m, p2], r3.at[m, p2], device))
     edge += send_edges(slice(0, 2))
-    unit = pl.ds(pl.multiple_of(p1 * thick + parity * 8, 8), 8)
-    back_sent = []
-    partner = ((x + 1 - 2 * parity) * nz + z, col)
+    gather = []
     for m in streams:
         for c in second_sent[m]:
             c.wait_recv()
         total = r3[m, 0]
         for a in range(1, n1):
             total = total + r3[m, a]
-        fresh[high + m, :, unit] = modes[high + m, :, unit] + total[:2] / (total[2:] + RELAX)
-        here = fresh.at[high + m, :, unit]
-        back_sent.append(copy(here, here, partner))
-    gather = []
-    for m in streams:
-        back_sent[m].wait_recv()
+        fresh[high + m, :, mine] = modes[high + m, :, mine] + total[:2] / (total[2:] + RELAX)
         here = fresh.at[high + m, :, mine]
         to_peers = {}
         for d in FAR:
             _, device = first_peer(d)
             to_peers[d] = copy(here, here, device)
         gather.append(to_peers)
+    late = [id(c) for to_peers in gather for c in to_peers.values()]
+    early = [c for c in pending if id(c) not in late]
     here = fresh.at[high + 1, :, mine]
     pair = [copy(here, here, sibling)]
 
@@ -446,6 +445,7 @@
         both_sums = centre(slice(0, 3), inner) + vertical + side
         new_object[:, part] = obj[:, part] + both_sums[:2] / (both_sums[2:] + RELAX)
 
+    flush(early)
     for d in NEAR:
         gather[0][d].wait_recv()
     pair.append(copy(fresh.at[high], fresh.at[high], sibling))
@@ -453,11 +453,10 @@
         gather[1][d].wait_recv()
         here = fresh.at[high + 1, :, chunk(lax.rem(p1 + n1 - d, n1))]
         pair.append(copy(here, here, sibling))
+    flush(list(gather[0].values()) + list(gather[1].values()))
     for c in pair:
         c.wait_recv()
-
-    for c in pending + pair_out:
-        c.wait_send()
+    flush(list(pair))
 
 
 def finish_kernel(object_in, fresh, object_out, modes_out, made, sem):
@@ -478,17 +477,20 @@
             br, bi = basis[j]
             vr = vr - (cr * br - ci * bi)
             vi = vi - (cr * bi + ci * br)
+        inner = {}
+        for later in range(k + 1, 4):
+            fr, fi = fresh[later, 0], fresh[later, 1]
+            inner[later] = (mean(vr * fr + vi * fi), mean(vr * fi - vi * fr))
         norm = 1.0 / jnp.sqrt(mean(vr * vr + vi * vi) + EPSILON)
         qr, qi = vr * norm, vi * norm
+        for later in range(k + 1, 4):
+            coefs[k, later] = (norm * inner[later][0], norm * inner[later][1])
         basis.append((qr, qi))
         made[k, 0] = qr
         made[k, 1] = qi
         write = pltpu.make_async_copy(made.at[k], modes_out.at[k], sem.at[k + 1])
         write.start()
         copies.append(write)
-        for later in range(k + 1, 4):
-            fr, fi = fresh[later, 0], fresh[later, 1]
-            coefs[k, later] = (mean(qr * fr + qi * fi), mean(qr * fi - qi * fr))
     for c in copies:
         c.wait()
 
@@ -501,7 +503,7 @@
 
     def body(object_field, amplitudes, counts, offsets, mode_index, mix_table, probe_modes):
         cap, mixes = amplitudes.shape[2], mix_table.shape[0]
-        number = 24 + 6 * (n1 - 1) + 2 * (nx - 1) + 2 + n1 + 1
+        number = 24 + 6 * (n1 - 1) + 2 * (nx - 1) + n1 + 1
         new_object, fresh = pl.pallas_call(
             functools.partial(kernel, rows, cols, nx, n1, cap, mixes),
             out_shape=(
@@ -541,8 +543,8 @@
                 pltpu.VMEM((2, 3, 128, 128), f32),
                 pltpu.VMEM((2, 3, 128, 128), f32),
                 pltpu.VMEM((2, n1 - 1, 3, 128 // n1, 128), f32),
-                pltpu.VMEM((2, 2 + nx, 3, 8, 128), f32),
-                pltpu.VMEM((2, n1, 3, 8, 128), f32),
+                pltpu.VMEM((2, nx, 3, 128 // n1, 128), f32),
+                pltpu.VMEM((2, n1, 3, 128 // n1, 128), f32),
                 pltpu.SemaphoreType.DMA((8,)),
                 pltpu.SemaphoreType.DMA((number,)),
                 pltpu.SemaphoreType.DMA((number,)),

time: 53.8 us -> 54.4 us (1.011)
  Pallas kernels: 52.4 us -> 53 us
    pallas_call x1, Pallas kernels: 50.8 us -> 51.7 us  [body(): pl.pallas_call(functools.partial(kernel, rows, cols, nx, n1, cap, mixes),...]
where the time goes in v7:
time: 54.4 us; the launch traced here: 54.3 us
  Pallas kernels  53 us (97%)
  between operations  1.28 us (2%)
    pallas_call x1, Pallas kernels, body(): pl.pallas_call(functools.partial(kernel, rows, cols, nx, n1, cap, mixes),...  51.7 us
    pallas_call x1, Pallas kernels, body(): pl.pallas_call(finish_kernel, out_shape=(jax.ShapeDtypeStruct((2, 128, 12...  1.31 us

profile of v7, /device:TPU:1, one launch (start us, length us, event | category | flops | bytes accessed | tf_op | source)
XLA Modules:
  0.0 54.3 jit_solution(13072527747892533181)
XLA Ops:
  1.3 51.7 %update.1 = (f32[2,128,128]{2,1,0:T(8,128)S(1)}, f32[4,2,128,128]{3,2,1,0:T(8,128)S(1)}) custom-call(f32[2,128,128]{2,1,0:T(8,128)} %o_hbm.1, bf16[1,1,12,128,128]{4,3,2,1,0:T(8,128)(2,1)} %a_hbm.1, s32[1,1]{1,0:T(1,128)S(6)} %copy.10.counts_hbm, s32[1,1,2,12]{3,2,1,0:T(2,128)} %bitcast.3, s32[1,1,12]{2,1,0:T(1,128)} %index_hbm.1, f32[4,16]{1,0:T(4,128)} %bitcast.2, ...), custom_call_target="tpu_custom_call" | custom-call | tf_op jit(solution)/shard_map/update/pallas_call | solution.py:507
  53.0 1.3 %finish.1 = (f32[2,128,128]{2,1,0:T(8,128)}, f32[4,2,128,128]{3,2,1,0:T(8,128)}) custom-call(f32[2,128,128]{2,1,0:T(8,128)S(1)} %get-tuple-element.4.object_in, f32[4,2,128,128]{3,2,1,0:T(8,128)S(1)} %get-tuple-element.5.fresh), custom_call_target="tpu_custom_call" | custom-call | tf_op jit(solution)/shard_map/finish/pallas_call | solution.py:562

commit v8 on v7

--- a/solution.py
+++ b/solution.py
@@ -294,18 +294,43 @@
 
     lane = lanes_iota((n, n))
 
+    thick = n // n1
+
+    def chunk(a):
+        return pl.ds(pl.multiple_of(a * thick, thick), thick)
+
+    def cut(step, carry):
+        for i in range(GROUP):
+            slot = step * GROUP + i
+            top, left_px = spot(slot)
+            mask = lane >= left_px
+            for comp in range(2):
+                a = tiles[comp, 0, pl.ds(top, n), :]
+                b = tiles[comp, 1, pl.ds(top, n), :]
+                patches[slot, comp] = pltpu.roll(jnp.where(mask, a, b), lax.rem(n - left_px, n), 1)
+        return carry
+
+    lax.fori_loop(0, cap // GROUP, cut, 0)
+
+    def weigh_rows(i, carry):
+        totals = [jnp.zeros((thick, n), jnp.float32) for _ in range(4)]
+        for slot in range(cap):
+            ar, ai = patches[slot, 0, chunk(i)], patches[slot, 1, chunk(i)]
+            value = ar * ar + ai * ai
+            for k in range(4):
+                totals[k] = totals[k] + splats[slot, 4 + k : 5 + k] * value
+        for k in range(4):
+            sums[k, 2, chunk(i)] = totals[k]
+        return carry
+
+    lax.fori_loop(0, n1, weigh_rows, 0)
+    dens_pair = copy(sums.at[pl.ds(other, 2), 2], got.at[:, 2], sibling)
+
     def visit(step, carry):
         slots = [step * TEAM + i for i in range(TEAM)]
         psi_r, psi_i = [], []
         for slot in slots:
-            top, left_px = spot(slot)
-            mask = lane >= left_px
-            patch = []
-            for comp in range(2):
-                a = tiles[comp, 0, pl.ds(top, n), :]
-                b = tiles[comp, 1, pl.ds(top, n), :]
-                patch.append(pltpu.roll(jnp.where(mask, a, b), lax.rem(n - left_px, n), 1))
-                patches[slot, comp] = patch[comp]
+            patch = (patches[slot, 0], patches[slot, 1])
             pr, pi = probes[slot, 0], probes[slot, 1]
             real = pr * patch[0] - pi * patch[1]
             imag = pr * patch[1] + pi * patch[0]
@@ -327,33 +352,34 @@
 
     lax.fori_loop(0, cap // TEAM, visit, 0)
 
-    thick = n // n1
-
-    def chunk(a):
-        return pl.ds(pl.multiple_of(a * thick, thick), thick)
+    dens_pair.wait_recv()
+    half[:, 2] = sums[pl.ds(high, 2), 2] + got[:, 2]
+    dens_first = []
+    for d in FAR:
+        a, device = first_peer(d)
+        dens_first.append(copy(half.at[:, 2, chunk(a)], r1.at[:, d - 1, 2], device))
 
     def pair_copy(i, d):
         piece = chunk(lax.rem(p2 + d, n1))
         return pltpu.make_async_remote_copy(
-            src_ref=sums.at[pl.ds(other, 2), :, piece], dst_ref=got.at[:, :, piece],
+            src_ref=sums.at[pl.ds(other, 2), 0:2, piece], dst_ref=got.at[:, 0:2, piece],
             send_sem=pair_send.at[i], recv_sem=pair_recv.at[i], device_id=sibling, device_id_type=MESH,
         )
 
     def finish_rows(i, carry):
         d = n1 // 2 + (1 - 2 * lax.rem(i, 2)) * ((i + 1) // 2)
         rows_here = chunk(lax.rem(p2 + d, n1))
-        totals = [[jnp.zeros((thick, n), jnp.float32) for _ in range(3)] for _ in range(4)]
+        totals = [[jnp.zeros((thick, n), jnp.float32) for _ in range(2)] for _ in range(4)]
         for slot in range(cap):
             dr, di = deltas[slot, 0, rows_here], deltas[slot, 1, rows_here]
             ar, ai = patches[slot, 0, rows_here], patches[slot, 1, rows_here]
-            pieces = (ar * dr + ai * di, ar * di - ai * dr, ar * ar + ai * ai)
+            pieces = (ar * dr + ai * di, ar * di - ai * dr)
             for k in range(4):
-                w, square = splats[slot, k : k + 1], splats[slot, 4 + k : 5 + k]
+                w = splats[slot, k : k + 1]
                 totals[k][0] = totals[k][0] + w * pieces[0]
                 totals[k][1] = totals[k][1] + w * pieces[1]
-                totals[k][2] = totals[k][2] + square * pieces[2]
         for k in range(4):
-            for f in range(3):
+            for f in range(2):
                 sums[k, f, rows_here] = totals[k][f]
         pair_copy(i, d).start()
         return carry
@@ -366,12 +392,12 @@
 
     def send_first(m, d):
         a, device = first_peer(d)
-        sent[m].append(copy(half.at[m, :, chunk(a)], r1.at[m, d - 1], device))
+        sent[m].append(copy(half.at[m, 0:2, chunk(a)], r1.at[m, d - 1, 0:2], device))
 
     for d, c in zip(order, pair_out):
         c.wait_recv()
         a, _ = first_peer(d)
-        half[:, :, chunk(a)] = sums[pl.ds(high, 2), :, chunk(a)] + got[:, :, chunk(a)]
+        half[:, 0:2, chunk(a)] = sums[pl.ds(high, 2), 0:2, chunk(a)] + got[:, 0:2, chunk(a)]
         if d:
             send_first(0, d)
     for d in FAR:
@@ -392,36 +418,59 @@
     flush(pair_out + halo + edge)
 
     mine = chunk(p1)
+    parity = lax.rem(x, 2)
+    total = half[:, 2, mine]
+    for d, c in zip(FAR[::-1], dens_first[::-1]):
+        c.wait_recv()
+        total = total + r1[:, d - 1, 2]
+    for t in range(2):
+        r2[:, t, 2] = total[:, t * 8 : (t + 1) * 8]
+    r2[:, 2 + x, 2] = r2[:, parity, 2]
+    dens_x = []
+    for d in range(1, nx):
+        a, device = x_peer(d)
+        dens_x.append(copy(r2.at[:, lax.rem(a, 2), 2], r2.at[:, 2 + x, 2], device))
     x_sent = [[], []]
     for m in streams:
-        total = half[m, :, mine]
+        total = half[m, 0:2, mine]
         for d, c in zip(FAR[::-1], sent[m][::-1]):
             c.wait_recv()
-            total = total + r1[m, d - 1]
-        r2[m, x] = total
+            total = total + r1[m, d - 1, 0:2]
+        for t in range(2):
+            r2[m, t, 0:2] = total[:, t * 8 : (t + 1) * 8]
+        r2[m, 2 + x, 0:2] = r2[m, parity, 0:2]
         for d in range(1, nx):
-            _, device = x_peer(d)
-            x_sent[m].append(copy(r2.at[m, x], r2.at[m, x], device))
+            a, device = x_peer(d)
+            x_sent[m].append(copy(r2.at[m, lax.rem(a, 2), 0:2], r2.at[m, 2 + x, 0:2], device))
+    for c in dens_x:
+        c.wait_recv()
     second_sent = [[], []]
     for m in streams:
         for c in x_sent[m]:
             c.wait_recv()
-        total = r2[m, 0]
+        total = r2[m, 2]
         for a in range(1, nx):
-            total = total + r2[m, a]
+            total = total + r2[m, 2 + a]
         r3[m, p2] = total
         for d in FAR:
             _, device = second_peer(d)
             second_sent[m].append(copy(r3.at[m, p2], r3.at[m, p2], device))
     edge += send_edges(slice(0, 2))
-    gather = []
+    unit = pl.ds(pl.multiple_of(p1 * thick + parity * 8, 8), 8)
+    back_sent = []
+    partner = ((x + 1 - 2 * parity) * nz + z, col)
     for m in streams:
         for c in second_sent[m]:
             c.wait_recv()
         total = r3[m, 0]
         for a in range(1, n1):
             total = total + r3[m, a]
-        fresh[high + m, :, mine] = modes[high + m, :, mine] + total[:2] / (total[2:] + RELAX)
+        fresh[high + m, :, unit] = modes[high + m, :, unit] + total[:2] / (total[2:] + RELAX)
+        here = fresh.at[high + m, :, unit]
+        back_sent.append(copy(here, here, partner))
+    gather = []
+    for m in streams:
+        back_sent[m].wait_recv()
         here = fresh.at[high + m, :, mine]
         to_peers = {}
         for d in FAR:
@@ -503,7 +552,7 @@
 
     def body(object_field, amplitudes, counts, offsets, mode_index, mix_table, probe_modes):
         cap, mixes = amplitudes.shape[2], mix_table.shape[0]
-        number = 24 + 6 * (n1 - 1) + 2 * (nx - 1) + n1 + 1
+        number = 25 + 7 * (n1 - 1) + 3 * (nx - 1) + 2 + n1 + 1
         new_object, fresh = pl.pallas_call(
             functools.partial(kernel, rows, cols, nx, n1, cap, mixes),
             out_shape=(
@@ -543,8 +592,8 @@
                 pltpu.VMEM((2, 3, 128, 128), f32),
                 pltpu.VMEM((2, 3, 128, 128), f32),
                 pltpu.VMEM((2, n1 - 1, 3, 128 // n1, 128), f32),
-                pltpu.VMEM((2, nx, 3, 128 // n1, 128), f32),
-                pltpu.VMEM((2, n1, 3, 128 // n1, 128), f32),
+                pltpu.VMEM((2, 2 + nx, 3, 8, 128), f32),
+                pltpu.VMEM((2, n1, 3, 8, 128), f32),
                 pltpu.SemaphoreType.DMA((8,)),
                 pltpu.SemaphoreType.DMA((number,)),
                 pltpu.SemaphoreType.DMA((number,)),

time: 54.4 us -> 54.4 us (level)
  no operation moved by 1% of the time
where the time goes in v8:
time: 54.4 us; the launch traced here: 54.3 us
  Pallas kernels  53 us (97%)
  between operations  1.28 us (2%)
    pallas_call x1, Pallas kernels, body(): pl.pallas_call(functools.partial(kernel, rows, cols, nx, n1, cap, mixes),...  51.7 us
    pallas_call x1, Pallas kernels, body(): pl.pallas_call(finish_kernel, out_shape=(jax.ShapeDtypeStruct((2, 128, 12...  1.31 us

profile of v8, /device:TPU:1, one launch (start us, length us, event | category | flops | bytes accessed | tf_op | source)
XLA Modules:
  0.0 54.3 jit_solution(18017619940724247216)
XLA Ops:
  1.3 51.7 %update.1 = (f32[2,128,128]{2,1,0:T(8,128)S(1)}, f32[4,2,128,128]{3,2,1,0:T(8,128)S(1)}) custom-call(f32[2,128,128]{2,1,0:T(8,128)} %o_hbm.1, bf16[1,1,12,128,128]{4,3,2,1,0:T(8,128)(2,1)} %a_hbm.1, s32[1,1]{1,0:T(1,128)S(6)} %copy.10.counts_hbm, s32[1,1,2,12]{3,2,1,0:T(2,128)} %bitcast.3, s32[1,1,12]{2,1,0:T(1,128)} %index_hbm.1, f32[4,16]{1,0:T(4,128)} %bitcast.2, ...), custom_call_target="tpu_custom_call" | custom-call | tf_op jit(solution)/shard_map/update/pallas_call | solution.py:556
  53.0 1.3 %finish.1 = (f32[2,128,128]{2,1,0:T(8,128)}, f32[4,2,128,128]{3,2,1,0:T(8,128)}) custom-call(f32[2,128,128]{2,1,0:T(8,128)S(1)} %get-tuple-element.4.object_in, f32[4,2,128,128]{3,2,1,0:T(8,128)S(1)} %get-tuple-element.5.fresh), custom_call_target="tpu_custom_call" | custom-call | tf_op jit(solution)/shard_map/finish/pallas_call | solution.py:611

commit v9 on v6

--- a/solution.py
+++ b/solution.py
@@ -127,6 +127,12 @@
         made.start()
         pending.append(made)
         return made
+
+    def flush(copies):
+        for c in copies:
+            c.wait_send()
+        done = [id(c) for c in copies]
+        pending[:] = [c for c in pending if id(c) not in done]
 
     def ok(dr, dc):
         return inside(row, col, rows, cols, dr, dc)
@@ -246,7 +252,7 @@
         return carry
 
     lax.fori_loop(0, cap // GROUP, make_probes, 0)
-    edge = send_edges(slice(2, 3))
+    edge = []
     for c in halo:
         c.wait_recv()
 
@@ -383,6 +389,7 @@
         return carry
 
     lax.fori_loop(0, cap // GROUP, numerators, 0)
+    flush(pair_out + halo + edge)
 
     mine = chunk(p1)
     parity = lax.rem(x, 2)
@@ -409,7 +416,7 @@
         for d in FAR:
             _, device = second_peer(d)
             second_sent[m].append(copy(r3.at[m, p2], r3.at[m, p2], device))
-    edge += send_edges(slice(0, 2))
+    edge += send_edges(slice(0, 3))
     unit = pl.ds(pl.multiple_of(p1 * thick + parity * 8, 8), 8)
     back_sent = []
     partner = ((x + 1 - 2 * parity) * nz + z, col)
@@ -431,6 +438,8 @@
             _, device = first_peer(d)
             to_peers[d] = copy(here, here, device)
         gather.append(to_peers)
+    late = [id(c) for to_peers in gather for c in to_peers.values()]
+    early = [c for c in pending if id(c) not in late]
     here = fresh.at[high + 1, :, mine]
     pair = [copy(here, here, sibling)]
 
@@ -446,6 +455,7 @@
         both_sums = centre(slice(0, 3), inner) + vertical + side
         new_object[:, part] = obj[:, part] + both_sums[:2] / (both_sums[2:] + RELAX)
 
+    flush(early)
     for d in NEAR:
         gather[0][d].wait_recv()
     pair.append(copy(fresh.at[high], fresh.at[high], sibling))
@@ -453,11 +463,10 @@
         gather[1][d].wait_recv()
         here = fresh.at[high + 1, :, chunk(lax.rem(p1 + n1 - d, n1))]
         pair.append(copy(here, here, sibling))
+    flush(list(gather[0].values()) + list(gather[1].values()))
     for c in pair:
         c.wait_recv()
-
-    for c in pending + pair_out:
-        c.wait_send()
+    flush(list(pair))
 
 
 def finish_kernel(object_in, fresh, object_out, modes_out, made, sem):
@@ -478,17 +487,20 @@
             br, bi = basis[j]
             vr = vr - (cr * br - ci * bi)
             vi = vi - (cr * bi + ci * br)
+        inner = {}
+        for later in range(k + 1, 4):
+            fr, fi = fresh[later, 0], fresh[later, 1]
+            inner[later] = (mean(vr * fr + vi * fi), mean(vr * fi - vi * fr))
         norm = 1.0 / jnp.sqrt(mean(vr * vr + vi * vi) + EPSILON)
         qr, qi = vr * norm, vi * norm
+        for later in range(k + 1, 4):
+            coefs[k, later] = (norm * inner[later][0], norm * inner[later][1])
         basis.append((qr, qi))
         made[k, 0] = qr
         made[k, 1] = qi
         write = pltpu.make_async_copy(made.at[k], modes_out.at[k], sem.at[k + 1])
         write.start()
         copies.append(write)
-        for later in range(k + 1, 4):
-            fr, fi = fresh[later, 0], fresh[later, 1]
-            coefs[k, later] = (mean(qr * fr + qi * fi), mean(qr * fi - qi * fr))
     for c in copies:
         c.wait()
 

time: 53.8 us -> 53 us (0.985)
  Pallas kernels: 52.4 us -> 51.6 us
    pallas_call x1, Pallas kernels: 50.8 us -> 50.3 us  [body(): pl.pallas_call(functools.partial(kernel, rows, cols, nx, n1, cap, mixes),...]
where the time goes in v9:
time: 53 us; the launch traced here: 52.8 us
  Pallas kernels  51.6 us (97%)
  between operations  1.28 us (2%)
    pallas_call x1, Pallas kernels, body(): pl.pallas_call(functools.partial(kernel, rows, cols, nx, n1, cap, mixes),...  50.3 us
    pallas_call x1, Pallas kernels, body(): pl.pallas_call(finish_kernel, out_shape=(jax.ShapeDtypeStruct((2, 128, 12...  1.31 us

profile of v9, /device:TPU:1, one launch (start us, length us, event | category | flops | bytes accessed | tf_op | source)
XLA Modules:
  0.0 52.8 jit_solution(16721233886499248461)
XLA Ops:
  1.3 50.3 %update.1 = (f32[2,128,128]{2,1,0:T(8,128)S(1)}, f32[4,2,128,128]{3,2,1,0:T(8,128)S(1)}) custom-call(f32[2,128,128]{2,1,0:T(8,128)} %o_hbm.1, bf16[1,1,12,128,128]{4,3,2,1,0:T(8,128)(2,1)} %a_hbm.1, s32[1,1]{1,0:T(1,128)S(6)} %copy.10.counts_hbm, s32[1,1,2,12]{3,2,1,0:T(2,128)} %bitcast.3, s32[1,1,12]{2,1,0:T(1,128)} %index_hbm.1, f32[4,16]{1,0:T(4,128)} %bitcast.2, ...), custom_call_target="tpu_custom_call" | custom-call | tf_op jit(solution)/shard_map/update/pallas_call | solution.py:517
  51.5 1.3 %finish.1 = (f32[2,128,128]{2,1,0:T(8,128)}, f32[4,2,128,128]{3,2,1,0:T(8,128)}) custom-call(f32[2,128,128]{2,1,0:T(8,128)S(1)} %get-tuple-element.4.object_in, f32[4,2,128,128]{3,2,1,0:T(8,128)S(1)} %get-tuple-element.5.fresh), custom_call_target="tpu_custom_call" | custom-call | tf_op jit(solution)/shard_map/finish/pallas_call | solution.py:572

commit v10 on v9

--- a/solution.py
+++ b/solution.py
@@ -16,6 +16,7 @@
 TEAM = 12
 FAR = (4, 3, 5, 2, 6, 1, 7)
 NEAR = (1, 7, 2, 6, 3, 5, 4)
+SIDE = (4, 3, 2, 5, 6, 1, 7)
 MESH = pl.DeviceIdType.MESH
 VMEM = pl.BlockSpec(memory_space=pltpu.VMEM)
 HBM = pl.BlockSpec(memory_space=pltpu.HBM)
@@ -374,7 +375,7 @@
         half[:, :, chunk(a)] = sums[pl.ds(high, 2), :, chunk(a)] + got[:, :, chunk(a)]
         if d:
             send_first(0, d)
-    for d in FAR:
+    for d in SIDE:
         send_first(1, d)
 
     def numerators(step, carry):
@@ -396,7 +397,7 @@
     x_sent = [[], []]
     for m in streams:
         total = half[m, :, mine]
-        for d, c in zip(FAR[::-1], sent[m][::-1]):
+        for d, c in zip((FAR, SIDE)[m][::-1], sent[m][::-1]):
             c.wait_recv()
             total = total + r1[m, d - 1]
         for t in range(2):
@@ -413,7 +414,7 @@
         for a in range(1, nx):
             total = total + r2[m, 2 + a]
         r3[m, p2] = total
-        for d in FAR:
+        for d in SIDE:
             _, device = second_peer(d)
             second_sent[m].append(copy(r3.at[m, p2], r3.at[m, p2], device))
     edge += send_edges(slice(0, 3))
@@ -434,7 +435,7 @@
         back_sent[m].wait_recv()
         here = fresh.at[high + m, :, mine]
         to_peers = {}
-        for d in FAR:
+        for d in SIDE:
             _, device = first_peer(d)
             to_peers[d] = copy(here, here, device)
         gather.append(to_peers)

time: 53 us -> 52.9 us (level)
  no operation moved by 1% of the time
where the time goes in v10:
time: 52.9 us; the launch traced here: 52.6 us
  Pallas kernels  51.4 us (97%)
  between operations  1.28 us (2%)
    pallas_call x1, Pallas kernels, body(): pl.pallas_call(functools.partial(kernel, rows, cols, nx, n1, cap, mixes),...  50 us
    pallas_call x1, Pallas kernels, body(): pl.pallas_call(finish_kernel, out_shape=(jax.ShapeDtypeStruct((2, 128, 12...  1.31 us

profile of v10, /device:TPU:1, one launch (start us, length us, event | category | flops | bytes accessed | tf_op | source)
XLA Modules:
  0.0 52.6 jit_solution(11152911002356052649)
XLA Ops:
  1.3 50.0 %update.1 = (f32[2,128,128]{2,1,0:T(8,128)S(1)}, f32[4,2,128,128]{3,2,1,0:T(8,128)S(1)}) custom-call(f32[2,128,128]{2,1,0:T(8,128)} %o_hbm.1, bf16[1,1,12,128,128]{4,3,2,1,0:T(8,128)(2,1)} %a_hbm.1, s32[1,1]{1,0:T(1,128)S(6)} %copy.10.counts_hbm, s32[1,1,2,12]{3,2,1,0:T(2,128)} %bitcast.3, s32[1,1,12]{2,1,0:T(1,128)} %index_hbm.1, f32[4,16]{1,0:T(4,128)} %bitcast.2, ...), custom_call_target="tpu_custom_call" | custom-call | tf_op jit(solution)/shard_map/update/pallas_call | solution.py:518
  51.3 1.3 %finish.1 = (f32[2,128,128]{2,1,0:T(8,128)}, f32[4,2,128,128]{3,2,1,0:T(8,128)}) custom-call(f32[2,128,128]{2,1,0:T(8,128)S(1)} %get-tuple-element.4.object_in, f32[4,2,128,128]{3,2,1,0:T(8,128)S(1)} %get-tuple-element.5.fresh), custom_call_target="tpu_custom_call" | custom-call | tf_op jit(solution)/shard_map/finish/pallas_call | solution.py:573
